TPU v7x, 32 devices: a whole 2x2x4 slice. The times are simulated.
32 devices in a mesh: chan: 16 (over z, x, core), band: 2 (over y).
Axes of the slice: x: 2, y: 2, z: 4, core: 2. Of those that a mesh axis runs over, the one named last changes fastest.
Arguments:
- raw: bfloat16 [1024, 4, 8192], P('chan', None, 'band')
- selection: int32 [512], P('chan'), may hold values from 0 to 63, as said below
- pairs: int32 [128, 2], P('chan'), may hold values from 0 to 15, as said below
Outputs:
- cross_spectra: bfloat16 [128, 32, 32, 2, 2048], P('chan', None, None, None, 'band')
Inputs may be any that keep to these rules, and one draw needn't show every extreme that they name: `selection`: each aligned group of 32 entries (one block) holds distinct indices of that block's recorded channels, always including 0 and 63. All rows are distinct pairs (i, j) of block numbers with i <= j; the first row is (0, last block).
All inputs are finite; a program needn't handle non-finite values.
Results may differ from a plain program's by a relative error of at most 0.0078.
Values may be sent and summed in bfloat16 or wider, within the bound.
No kernel may reach another device: no remote copies, remote signals or barrier semaphores. Data moves between devices by JAX's collectives and lax.ppermute only.
A program may use at most 256 MiB of HBM per device.

v0:
```python
import functools
import math

import numpy as np

import jax
import jax.numpy as jnp
from jax import lax
from jax.experimental import pallas as pl
from jax.experimental.pallas import tpu as pltpu
from jax.sharding import PartitionSpec as P

WIN = 4
L = 4096
F = 2048
DEC = 2
TAPS = 16
RADIUS = 8
EPSILON = 1e-06
LANES = 128
CHUNKS = (16, 16)
TILE = (4, 32)
PIECE = 4
TURNS = 4
VMEM_CROSS = 56
MIB = 2**20


def fir_numpy():
    position = np.arange(TAPS, dtype=np.float64)
    shaped = np.sinc((position - (TAPS - 1) / 2.0) / DEC)
    shaped = shaped * (0.5 - 0.5 * np.cos(2.0 * math.pi * (position + 0.5) / TAPS))
    return shaped / shaped.sum()


def high_low(matrix):
    exact = matrix.astype(np.float32)
    high = exact.astype(jnp.bfloat16)
    low = (exact - high.astype(np.float32)).astype(jnp.bfloat16)
    return np.concatenate([high, low], axis=1)


def fir_matrices():
    taps = fir_numpy()
    inner = np.zeros((3 * LANES, LANES))
    first = np.zeros((LANES, LANES))
    for out in range(LANES):
        for tap in range(TAPS):
            sample = DEC * out - tap
            inner[LANES + sample, out] = taps[tap]
            if out < TAPS // DEC:
                first[sample % LANES, out] = taps[tap]
    return high_low(inner), high_low(first)


def trig_tables(band_count, bins_dev, length):
    angle = 2.0 * math.pi * np.arange(L) / L
    cosine = np.cos(angle).astype(np.float32).astype(jnp.bfloat16)
    sine = (-np.sin(angle)).astype(np.float32).astype(jnp.bfloat16)
    times = np.arange(length)
    tiles = bins_dev // LANES
    table = np.zeros((band_count, tiles + 1, length, 2 * LANES), jnp.bfloat16)
    for band in range(band_count):
        for tile in range(tiles + 1):
            lane = np.arange(LANES)
            if tile < tiles:
                bins = band * bins_dev + tile * LANES + lane
                keep = lane >= 0
            else:
                bins = np.where(lane < LANES // 2, (band + 1) * bins_dev + lane, band * bins_dev - LANES + lane)
                keep = ((lane < RADIUS) | (lane >= LANES - RADIUS)) & (bins >= 0) & (bins < F)
            phase = (times[:, None] * bins[None, :]) % L
            table[band, tile, :, :LANES] = np.where(keep[None, :], cosine[phase], 0)
            table[band, tile, :, LANES:] = np.where(keep[None, :], sine[phase], 0)
    return table


def two_products(samples, matrix):
    both = jnp.dot(samples, matrix, preferred_element_type=jnp.float32)
    return both[:, :LANES] + both[:, LANES:]


def decimate_kernel(order_ref, raw_ref, inner_ref, out_ref):
    rows, samples = raw_ref.shape
    order = order_ref[...]

    def put(first_lane, value):
        moved = jnp.dot(order, value, preferred_element_type=jnp.float32)
        out_ref[:, first_lane : first_lane + value.shape[1]] = moved.astype(jnp.bfloat16)

    blocks = samples // (2 * LANES)
    for block in range(0, blocks, 2):
        pair = []
        for b in (block, block + 1):
            start = 2 * LANES * b - LANES
            if b == 0:
                value = two_products(raw_ref[:, 0 : 2 * LANES], inner_ref[LANES:, :])
            else:
                value = two_products(raw_ref[:, start : start + 3 * LANES], inner_ref[...])
            pair.append(value.astype(jnp.bfloat16))
        put(block * LANES, jnp.concatenate(pair, axis=1))
    lane = lax.broadcasted_iota(jnp.int32, (rows, LANES), 1)
    edge = jnp.where(
        lane < LANES // 2,
        raw_ref[:, 0:LANES].astype(jnp.float32),
        raw_ref[:, samples - LANES :].astype(jnp.float32),
    ).astype(jnp.bfloat16)
    put(blocks * LANES, edge)


def whiten_kernel(band_ref, own_ref, other_ref, first_ref, table_ref, *refs):
    chunk_refs = refs[: len(CHUNKS)]
    halves_ref, spectra_ref, spread_ref, tiles_ref, table_sem = refs[len(CHUNKS) :]
    tiles = tiles_ref.shape[0]

    def tile_copy(tile):
        return pltpu.make_async_copy(table_ref.at[band_ref[0], tile], tiles_ref.at[tile], table_sem.at[tile])

    for tile in range(tiles):
        tile_copy(tile).start()
    rows = own_ref.shape[0]
    channels = rows // WIN
    length = halves_ref.shape[1]
    lane = lax.broadcasted_iota(jnp.int32, (rows, LANES), 1)

    def gather(earlier, later):
        halves_ref[:rows, :] = earlier[:, :length]
        halves_ref[rows:, :] = later[:, :length]
        window = jnp.where(
            lane < LANES // 2,
            later[:, length:].astype(jnp.float32),
            earlier[:, length:].astype(jnp.float32),
        ).astype(jnp.bfloat16)
        fixed = two_products(window, first_ref[...])
        halves_ref[rows:, :LANES] = jnp.where(
            lane < TAPS // DEC, fixed, later[:, :LANES].astype(jnp.float32)
        ).astype(jnp.bfloat16)

    @pl.when(band_ref[0] == 0)
    def _():
        gather(own_ref, other_ref)

    @pl.when(band_ref[0] != 0)
    def _():
        gather(other_ref, own_ref)

    odd = lax.broadcasted_iota(jnp.int32, (rows, 2 * LANES), 1) % 2 == 1

    def transform(tile, _):
        tile_copy(tile).wait()
        both = jnp.dot(halves_ref[...], tiles_ref[tile], preferred_element_type=jnp.float32)
        later = both[rows:]
        spectra_ref[tile] = both[:rows] + jnp.where(odd, -later, later)
        return 0

    lax.fori_loop(0, tiles, transform, 0)
    count = spectra_ref.shape[0] - 1
    power = []
    for t in range(count + 1):
        total = jnp.zeros((channels, LANES), jnp.float32)
        for w in range(WIN):
            for part in range(2):
                v = spectra_ref[t, w * channels : (w + 1) * channels, part * LANES : (part + 1) * LANES]
                total = total + v * v
        power.append(total)
    around = jnp.concatenate([power[count]] + power[:count] + [power[count]], axis=1)
    width = around.shape[1]
    sums = around
    for step in (1, 2, 4, 8):
        sums = sums + pltpu.roll(sums, step, 1)
    sums = sums + pltpu.roll(around, 2 * RADIUS, 1)
    sums = pltpu.roll(sums, width - RADIUS, 1)
    scale = lax.rsqrt(sums / (WIN * (2 * RADIUS + 1)) + EPSILON)
    for t in range(count):
        factor = scale[:, (t + 1) * LANES : (t + 2) * LANES]
        for w in range(WIN):
            for part in range(2):
                value = (
                    spectra_ref[t, w * channels : (w + 1) * channels, part * LANES : (part + 1) * LANES]
                    * factor
                )
                for c in range(0, channels, 8):
                    base = (c * WIN + w) * 8 + 2 * (t % 4) + part
                    spread_ref[t // 4, pl.ds(base, 8, stride=8 * WIN), :] = value[c : c + 8]
    first = 0
    for chunk_ref in chunk_refs:
        size = chunk_ref.shape[1]
        sides = [spread_ref[k, first : first + size] for k in range(count // 4)]
        chunk_ref[0] = jnp.concatenate(sides, axis=1).astype(jnp.bfloat16)
        first += size


def cross_kernel(pairs_ref, slot_ref, *refs):
    gathered, refs = refs[: len(CHUNKS)], refs[len(CHUNKS) :]
    out_ref, blocks_ref, planes_ref, result_ref, block_sem, out_sem = refs
    count = out_ref.shape[0]
    channels = planes_ref.shape[2]
    row_step, col_step = TILE
    groups = channels // row_step
    col_steps = channels // col_step
    ahead = channels // (groups * col_steps)
    turns = result_ref.shape[0]
    rows = WIN * 8

    def fetches(pair, s):
        copies = []
        for side in range(2):
            first = 0
            for k, from_ref in enumerate(gathered):
                size = from_ref.shape[1]
                copies.append(
                    pltpu.make_async_copy(
                        from_ref.at[slot_ref[pairs_ref[pair, side]]],
                        blocks_ref.at[s, side, pl.ds(first, size)],
                        block_sem.at[s, side, k],
                    )
                )
                first += size
        return copies

    lanes = planes_ref.shape[5]
    row = lax.broadcasted_iota(jnp.int32, (8, lanes), 0)
    sign = jnp.where(row % 2 == 0, 1.0, -1.0).astype(jnp.bfloat16)

    def prepare(s, c):
        first = pl.multiple_of(c * rows, rows)
        row_block = blocks_ref[s, 0, pl.ds(first, rows)].astype(jnp.float32)
        col_block = blocks_ref[s, 1, pl.ds(first, rows)].astype(jnp.float32)
        for w in range(WIN):
            value = row_block[8 * w : 8 * w + 8]
            turned = jnp.take_along_axis(value, row + 1 - 2 * (row % 2), axis=0)
            planes_ref[s, 0, c, w] = value.astype(jnp.bfloat16)
            planes_ref[s, 1, c, w] = turned.astype(jnp.bfloat16) * sign
            value = col_block[8 * w : 8 * w + 8]
            planes_ref[s, 2, c, w] = jnp.take_along_axis(value, row - row % 2, axis=0).astype(jnp.bfloat16)
            planes_ref[s, 3, c, w] = jnp.take_along_axis(value, row + 1 - row % 2, axis=0).astype(jnp.bfloat16)

    def store(pair, turn, group):
        return pltpu.make_async_copy(
            result_ref.at[turn], out_ref.at[pair, pl.ds(group * row_step, row_step)], out_sem.at[turn]
        )

    def first_pair(c, _):
        prepare(0, c)
        return 0

    for pair in range(2):
        for copy in fetches(pair, pair):
            copy.start()
    for copy in fetches(0, 0):
        copy.wait()
    lax.fori_loop(0, channels, first_pair, 0)

    def piece(s, turn, a0, a, b0):
        total = [[None] * PIECE for _ in range(PIECE)]
        for w in range(WIN):
            straight = [planes_ref[s, 0, a0 + a + k, w] for k in range(PIECE)]
            turned = [planes_ref[s, 1, a0 + a + k, w] for k in range(PIECE)]
            for m in range(PIECE):
                real, imag = planes_ref[s, 2, b0 + m, w], planes_ref[s, 3, b0 + m, w]
                for k in range(PIECE):
                    term = straight[k] * real + turned[k] * imag
                    total[k][m] = term if w == 0 else total[k][m] + term
        for k in range(PIECE):
            for m in range(PIECE):
                result_ref[turn, a + k, b0 + m, 0:8] = total[k][m][:, :LANES]
                result_ref[turn, a + k, b0 + m, 8:16] = total[k][m][:, LANES:]

    def one_pair(pair, _):
        s = lax.rem(pair, 2)

        @pl.when(pair + 2 < count)
        def _():
            for copy in fetches(pair + 2, s):
                copy.start()

        @pl.when(pair + 1 < count)
        def _():
            for copy in fetches(pair + 1, 1 - s):
                copy.wait()

        def one_group(group, _):
            a0 = group * row_step
            turn = lax.rem(pair * groups + group, turns)

            @pl.when(pair * groups + group >= turns)
            def _():
                store(0, turn, 0).wait()

            def one(step, _):
                b0 = step * col_step
                for k in range(ahead):
                    prepare(1 - s, (group * col_steps + step) * ahead + k)
                for a in range(0, row_step, PIECE):
                    for b in range(0, col_step, PIECE):
                        piece(s, turn, a0, a, b0 + b)
                return 0

            lax.fori_loop(0, col_steps, one, 0)
            store(pair, turn, group).start()
            return 0

        lax.fori_loop(0, groups, one_group, 0)
        return 0

    lax.fori_loop(0, count, one_pair, 0)
    for turn in range(turns):
        store(0, turn, 0).wait()


def cross_spectra(pairs, slots, gathered):
    pair_count = pairs.shape[0]
    channels = sum(CHUNKS)
    lanes = gathered[0].shape[2]
    smem = pl.BlockSpec(memory_space=pltpu.SMEM)
    hbm = pl.BlockSpec(memory_space=pl.ANY)
    return pl.pallas_call(
        cross_kernel,
        in_specs=[smem, smem] + [hbm] * len(gathered),
        out_specs=hbm,
        scratch_shapes=[
            pltpu.VMEM((2, 2, channels * WIN * 8, lanes), jnp.bfloat16),
            pltpu.VMEM((2, 4, channels, WIN, 8, lanes), jnp.bfloat16),
            pltpu.VMEM((TURNS, TILE[0], channels, 16, LANES), jnp.bfloat16),
            pltpu.SemaphoreType.DMA((2, 2, len(gathered))),
            pltpu.SemaphoreType.DMA((TURNS,)),
        ],
        out_shape=jax.ShapeDtypeStruct((pair_count, channels, channels, 16, LANES), jnp.bfloat16),
        compiler_params=pltpu.CompilerParams(vmem_limit_bytes=VMEM_CROSS * MIB),
        name="cross_spectra",
    )(pairs, slots, *gathered)


def ring_positions(mesh):
    depth = mesh.shape["chan"] // 4
    plane = [(z, 0) for z in range(depth)] + [(z, 1) for z in reversed(range(depth))]
    return [[(z * 2 + x) * 2 + core for core in range(2)] for z, x in plane]


def reserve(shape):
    def nothing(out_ref):
        del out_ref

    return pl.pallas_call(
        nothing,
        out_specs=pl.BlockSpec(memory_space=pl.ANY),
        out_shape=jax.ShapeDtypeStruct(shape, jnp.bfloat16),
        name="reserve",
    )()


def gather_blocks(chunks, swap, ring):
    move = functools.partial(lax.ppermute, axis_name="chan")
    count = len(ring)
    gathered = [reserve((count,) + own.shape[1:]) for own in chunks]

    def put(k, piece, slot):
        gathered[k] = lax.dynamic_update_slice(gathered[k], piece, (slot, 0, 0))

    current = [jnp.concatenate([own, move(own, perm=swap)], axis=0) for own in chunks]
    for k, piece in enumerate(current):
        put(k, piece, 0)
    steps = count // 4
    for step in range(1, steps + 1):
        for k in range(len(chunks)):
            current[k] = move(current[k][:1] if step == steps else current[k], perm=ring)
            put(k, current[k], 4 * step - 2)
            put(k, move(current[k], perm=swap), 4 * step - (1 if step == steps else 0))
    return gathered


def slot_table(positions):
    count = len(positions)
    table = np.zeros((2 * count, 2 * count), np.int32)
    for q in range(count):
        for core in range(2):

            def received(c, step):
                chip = positions[(q - step) % count] if c == 0 else positions[(q + step) % count]
                return [chip[c], chip[1 - c]]

            order = received(core, 0)
            for step in range(1, count // 2):
                order += received(core, step) + received(1 - core, step)
            order += received(core, count // 2)[:1] + received(1 - core, count // 2)[:1]
            table[positions[q][core], order] = np.arange(2 * count)
    return table


def body(positions, raw, selection, pairs):
    channels = selection.shape[0]
    rows = channels * WIN
    samples = raw.shape[2]
    length = samples // DEC
    bins_dev = F // 2
    tiles = bins_dev // LANES
    band = lax.axis_index("band").reshape(1)
    inner, first = fir_matrices()
    table = jnp.asarray(trig_tables(2, bins_dev, length))
    order = np.zeros((rows, rows), jnp.bfloat16)
    for window in range(WIN):
        for channel in range(channels):
            order[window * channels + channel, channel * WIN + window] = 1

    picked = raw.at[selection].get(mode="promise_in_bounds").reshape(rows, samples)
    message = pl.pallas_call(
        decimate_kernel,
        out_shape=jax.ShapeDtypeStruct((rows, length + LANES), jnp.bfloat16),
        compiler_params=pltpu.CompilerParams(vmem_limit_bytes=24 * MIB),
        name="decimate",
    )(jnp.asarray(order), picked, jnp.asarray(inner))
    other = lax.ppermute(message, "band", [(0, 1), (1, 0)])

    vmem = pl.BlockSpec(memory_space=pltpu.VMEM)
    chunk_shapes = [(1, size * WIN * 8, tiles // 4 * LANES) for size in CHUNKS]
    chunks = pl.pallas_call(
        whiten_kernel,
        in_specs=[pl.BlockSpec(memory_space=pltpu.SMEM), vmem, vmem, vmem, pl.BlockSpec(memory_space=pltpu.HBM)],
        out_specs=[vmem] * len(CHUNKS),
        scratch_shapes=[
            pltpu.VMEM((2 * rows, length), jnp.bfloat16),
            pltpu.VMEM((tiles + 1, rows, 2 * LANES), jnp.float32),
            pltpu.VMEM((tiles // 4, rows * 8, LANES), jnp.float32),
            pltpu.VMEM(table.shape[1:], jnp.bfloat16),
            pltpu.SemaphoreType.DMA((tiles + 1,)),
        ],
        out_shape=[jax.ShapeDtypeStruct(shape, jnp.bfloat16) for shape in chunk_shapes],
        compiler_params=pltpu.CompilerParams(vmem_limit_bytes=50 * MIB),
        name="whiten",
    )(band, message, other, jnp.asarray(first), table)

    count = len(positions)
    swap = [(chip[c], chip[1 - c]) for chip in positions for c in range(2)]
    ring = [(positions[q][0], positions[(q + 1) % count][0]) for q in range(count)]
    ring += [(positions[q][1], positions[(q - 1) % count][1]) for q in range(count)]
    slots = jnp.asarray(slot_table(positions))[lax.axis_index("chan")]
    result = cross_spectra(pairs, slots, gather_blocks(chunks, swap, ring))
    pair_count = pairs.shape[0]
    result = result.reshape(pair_count, channels, channels, tiles, 2, LANES)
    return result.transpose(0, 1, 2, 4, 3, 5).reshape(pair_count, channels, channels, 2, bins_dev)


def from_behind(block, axis, distance):
    devices = range(lax.axis_size(axis))
    route = [(i - distance, i) for i in devices if i - distance in devices]
    return lax.ppermute(block, axis, route)


def extended(block, sides, width):
    for axis, dim in sides:
        count = lax.axis_size(axis)
        forward = [(i, i + 1) for i in range(count - 1)]
        backward = [(target, source) for source, target in forward]
        low = lax.ppermute(
            lax.slice_in_dim(block, block.shape[dim] - width, None, axis=dim), axis, forward
        )
        high = lax.ppermute(lax.slice_in_dim(block, 0, width, axis=dim), axis, backward)
        block = jnp.concatenate([low, block, high], axis=dim)
    return block


def fir_taps(tap_count, factor):
    position = jnp.arange(tap_count, dtype=jnp.float32)
    centre = (tap_count - 1) / 2.0
    sinc_part = jnp.sinc((position - centre) / factor)
    hann_part = 0.5 - 0.5 * jnp.cos(2.0 * math.pi * (position + 0.5) / tap_count)
    shaped = sinc_part * hann_part
    return shaped / jnp.sum(shaped)


def tap_matrix(sample_pos, length, fir_coef):
    out_times = lax.iota(jnp.int32, length)
    tap_of = DEC * out_times[None, :] - sample_pos[:, None]
    matrix = jnp.zeros((sample_pos.shape[0], length), jnp.float32)
    for tap_index in range(TAPS):
        matrix = matrix + jnp.where(tap_of == tap_index, fir_coef[tap_index], 0.0)
    return matrix


def plain_trig_tables(freq_rows, first_time, time_count):
    step_fine = 64 if time_count % 64 == 0 else time_count
    coarse_count = time_count // step_fine
    coarse_times = first_time + step_fine * lax.iota(jnp.int32, coarse_count)
    fine_times = lax.iota(jnp.int32, step_fine)
    scale = 2.0 * math.pi / L
    coarse_angle = (freq_rows[:, None] * coarse_times[None, :] % L).astype(jnp.float32) * scale
    fine_angle = (freq_rows[:, None] * fine_times[None, :] % L).astype(jnp.float32) * scale
    cos_hi = jnp.cos(coarse_angle)[:, :, None]
    sin_hi = jnp.sin(coarse_angle)[:, :, None]
    cos_lo = jnp.cos(fine_angle)[:, None, :]
    sin_lo = jnp.sin(fine_angle)[:, None, :]
    rows = freq_rows.shape[0]
    cosine = (cos_hi * cos_lo - sin_hi * sin_lo).reshape(rows, time_count).astype(jnp.bfloat16)
    sine = (sin_hi * cos_lo + cos_hi * sin_lo).reshape(rows, time_count).astype(jnp.bfloat16)
    return (cosine, sine)


def spectrum_block(freq_rows, first_time, samples):
    cosine, sine = plain_trig_tables(freq_rows, first_time, samples.shape[1])
    contract = (((1,), (1,)), ((), ()))
    real_part = lax.dot_general(cosine, samples, contract, preferred_element_type=jnp.float32)
    imag_part = -lax.dot_general(sine, samples, contract, preferred_element_type=jnp.float32)
    return jnp.concatenate([real_part, imag_part], axis=1)


def plain_body(raw, selection, pairs):
    picked = jnp.take(raw, selection, axis=0)
    channels = picked.shape[0]
    samples_dev = picked.shape[2]
    row_total = channels * WIN
    tail_part = picked[:, :, samples_dev - (TAPS - 1) :]
    before = from_behind(tail_part, "band", 1)
    length = samples_dev // DEC
    fir_coef = fir_taps(TAPS, DEC)
    main_matrix = tap_matrix(lax.iota(jnp.int32, samples_dev), length, fir_coef)
    rim_matrix = tap_matrix(lax.iota(jnp.int32, TAPS - 1) - (TAPS - 1), length, fir_coef)
    main_rows = picked.reshape(row_total, samples_dev).astype(jnp.float32)
    rim_rows = before.reshape(row_total, TAPS - 1).astype(jnp.float32)
    decimated = jnp.dot(main_rows, main_matrix, precision=lax.Precision.HIGHEST)
    decimated = decimated + jnp.dot(rim_rows, rim_matrix, precision=lax.Precision.HIGHEST)
    flat_samples = decimated.astype(jnp.bfloat16)
    band_size = lax.axis_size("band")
    bins_dev = F // band_size
    first_time = lax.axis_index("band") * length
    freq_block = 256

    def one_block(first_freq):
        return spectrum_block(
            first_freq + lax.iota(jnp.int32, freq_block), first_time, flat_samples
        )

    first_freqs = freq_block * lax.iota(jnp.int32, lax.axis_size("band") * bins_dev // freq_block)
    spectra = lax.psum_scatter(
        lax.map(one_block, first_freqs).reshape(lax.axis_size("band") * bins_dev, 2 * row_total),
        "band",
        scatter_dimension=0,
        tiled=True,
    )
    spectra = spectra.reshape(bins_dev, 2, channels, WIN)
    power_sum = jnp.sum(spectra * spectra, axis=(1, 3))
    rimmed = extended(power_sum.astype(jnp.bfloat16), (("band", 0),), RADIUS).astype(
        power_sum.dtype
    )
    smooth = rimmed[0:bins_dev]
    for offset in range(1, 2 * RADIUS + 1):
        smooth = smooth + rimmed[offset : offset + bins_dev]
    whiten_scale = 1.0 / jnp.sqrt(smooth / (WIN * (2 * RADIUS + 1)) + EPSILON)
    whitened = (spectra * whiten_scale[:, None, :, None]).astype(jnp.bfloat16)
    whitened = jnp.transpose(whitened, (2, 3, 1, 0))
    pair_count = pairs.shape[0]
    empty = jnp.zeros((pair_count,) + whitened.shape, jnp.bfloat16)
    shard_piece = lax.all_gather(whitened, "chan", axis=0, tiled=True)
    shard_count = shard_piece.shape[0] // channels
    flat_blocks = shard_piece.reshape(shard_count, -1)
    block_index = jnp.int32(0) // channels + lax.iota(jnp.int32, shard_count)

    def select(hit_mask, previous):
        gathered = jnp.dot(
            hit_mask.astype(jnp.bfloat16), flat_blocks, preferred_element_type=jnp.float32
        )
        gathered = gathered.astype(jnp.bfloat16).reshape(previous.shape)
        any_hit = jnp.any(hit_mask, axis=1)
        return jnp.where(any_hit[:, None, None, None, None], gathered, previous)

    row_mask = pairs[:, 0:1] == block_index[None, :]
    col_mask = pairs[:, 1:2] == block_index[None, :]
    first_side = select(row_mask, empty)
    second_side = select(col_mask, empty)
    flipped = jnp.stack([-second_side[:, :, :, 1], second_side[:, :, :, 0]], axis=3)
    paired = jnp.stack([second_side, flipped], axis=3)
    cross_sum = jnp.einsum(
        "pawrf,pbwsrf->pabsf", first_side, paired, preferred_element_type=jnp.float32
    )
    return cross_sum.astype(jnp.bfloat16)


def solution(mesh):
    placed = (P("chan", None, "band"), P("chan"), P("chan", None))
    if mesh.shape["band"] == 2 and mesh.shape["chan"] == 16:
        inner = functools.partial(body, ring_positions(mesh))
    else:
        inner = plain_body
    return jax.shard_map(
        inner,
        mesh=mesh,
        in_specs=placed,
        out_specs=P("chan", None, None, None, "band"),
        check_vma=False,
    )
```

profile of v0, /device:TPU:1, one launch (start us, length us, event | category | flops | bytes accessed | tf_op | source)
XLA Modules:
  0.0 102.4 jit_solution(5098886668243799067)
XLA Ops:
  0.0 0.0 copy-start.3
  0.0 0.8 compare_select_fusion
  0.8 0.8 copy-done
  1.6 1.4 %gather_fusion = bf16[32,4,4096]{2,1,0:T(4,128)(2,1)S(1)} fusion(bf16[64,4,4096]{2,1,0:T(4,128)(2,1)S(1)} %copy-done, s32[1024]{0:T(1024)S(1)} %pad_clamp_fusion), kind=kCustom, calls=%fused_computation | custom fusion | bytes 2097280 | tf_op jit(solution)/shard_map/gather | solution.py:405
  3.1 0.3 reshape.13.raw_ref
  3.4 1.9 %decimate.1.own_ref = bf16[128,2176]{1,0:T(8,128)(2,1)S(1)} custom-call(bf16[128,128]{1,0:T(8,128)(2,1)S(1)} %copy-done.4, bf16[128,4096]{1,0:T(8,128)(2,1)S(1)} %reshape.13.raw_ref, bf16[384,256]{1,0:T(8,128)(2,1)S(1)} %copy-done.2), custom_call_target="tpu_custom_call" | custom-call | tf_op jit(solution)/shard_map/decimate/pallas_call | solution.py:406
  5.3 2.1 %collective-permute-start = (bf16[128,2176]{1,0:T(8,128)(2,1)S(1)}, bf16[128,2176]{1,0:T(8,128)(2,1)S(1)}, u32[]{:S(2)}, u32[]{:S(2)}) collective-permute-start(bf16[128,2176]{1,0:T(8,128)(2,1)S(1)} %decimate.1.own_ref), channel_id=1, source_target_pairs={{0,1},{1,0},{2,3},{3,2},{4,5},{5,4},{6,7},{7,6},{8,9},{9,8},{10,11... | collective-permute-start | bytes 1671176 | tf_op jit(solution)/shard_map/ppermute | solution.py:412
  7.4 12.4 %collective-permute-done.other_ref = bf16[128,2176]{1,0:T(8,128)(2,1)S(1)} collective-permute-done((bf16[128,2176]{1,0:T(8,128)(2,1)S(1)}, bf16[128,2176]{1,0:T(8,128)(2,1)S(1)}, u32[]{:S(2)}, u32[]{:S(2)}) %collective-permute-start) | collective-permute-done | bytes 557088 | tf_op jit(solution)/shard_map/ppermute | solution.py:412
  19.8 6.5 %whiten.1 = (bf16[1,512,256]{2,1,0:T(8,128)(2,1)S(1)}, bf16[1,512,256]{2,1,0:T(8,128)(2,1)S(1)}) custom-call(s32[1]{0:T(128)} %bitcast.1.band_ref, bf16[128,2176]{1,0:T(8,128)(2,1)S(1)} %decimate.1.own_ref, bf16[128,2176]{1,0:T(8,128)(2,1)S(1)} %collective-permute-done.other_ref, bf16[128,256]{1,0:T(8,128)(2,1)S(1)} %copy-done.3, ...), custom_call_target="tpu_custom_call" | custom-call | tf_op jit(solution)/shard_map/whiten/pallas_call | solution.py:416
  26.3 1.3 %collective-permute-start.10 = (bf16[1,512,256]{2,1,0:T(8,128)(2,1)S(1)}, bf16[1,512,256]{2,1,0:T(8,128)(2,1)S(1)}, u32[]{:S(2)}, u32[]{:S(2)}) collective-permute-start(bf16[1,512,256]{2,1,0:T(8,128)(2,1)S(1)} %get-tuple-element.8), channel_id=1, source_target_pairs={{0,2},{2,0},{8,10},{10,8},{16,18},{18,16},{24,26},{26,24},{28,30},... | collective-permute-start | bytes 786440 | tf_op jit(solution)/shard_map/ppermute | solution.py:360
  27.6 0.1 collective-permute-start.1
  27.7 1.1 %collective-permute-done.10 = bf16[1,512,256]{2,1,0:T(8,128)(2,1)S(1)} collective-permute-done((bf16[1,512,256]{2,1,0:T(8,128)(2,1)S(1)}, bf16[1,512,256]{2,1,0:T(8,128)(2,1)S(1)}, u32[]{:S(2)}, u32[]{:S(2)}) %collective-permute-start.10) | collective-permute-done | bytes 262176 | tf_op jit(solution)/shard_map/ppermute | solution.py:360
  28.7 1.5 %collective-permute-start.11 = (bf16[2,512,256]{2,1,0:T(8,128)(2,1)S(1)}, bf16[2,512,256]{2,1,0:T(8,128)(2,1)}, u32[]{:S(2)}, u32[]{:S(2)}) collective-permute-start(bf16[2,512,256]{2,1,0:T(8,128)(2,1)S(1)} %constant_dynamic-update-slice_fusion.2), channel_id=1, source_target_pairs={{0,8},{8,16},{16,24},{24,28},{28,20},{20,12},{12,4},{4,0},{2,6},{1... | collective-permute-start | bytes 1572872 | tf_op jit(solution)/shard_map/ppermute | solution.py:366
  30.3 0.0 collective-permute-done.1
  30.3 1.3 %collective-permute-start.2 = (bf16[2,512,256]{2,1,0:T(8,128)(2,1)S(1)}, bf16[2,512,256]{2,1,0:T(8,128)(2,1)S(1)}, u32[]{:S(2)}, u32[]{:S(2)}) collective-permute-start(bf16[2,512,256]{2,1,0:T(8,128)(2,1)S(1)} %constant_dynamic-update-slice_fusion), channel_id=1, source_target_pairs={{0,8},{8,16},{16,24},{24,28},{28,20},{20,12},{12,4},{4,0},{2,6},{1... | collective-permute-start | bytes 1572872 | tf_op jit(solution)/shard_map/ppermute | solution.py:366
  31.6 5.7 %collective-permute-done.11 = bf16[2,512,256]{2,1,0:T(8,128)(2,1)} collective-permute-done((bf16[2,512,256]{2,1,0:T(8,128)(2,1)S(1)}, bf16[2,512,256]{2,1,0:T(8,128)(2,1)}, u32[]{:S(2)}, u32[]{:S(2)}) %collective-permute-start.11) | collective-permute-done | bytes 524320 | tf_op jit(solution)/shard_map/ppermute | solution.py:366
  37.3 1.4 %collective-permute-start.13 = (bf16[2,512,256]{2,1,0:T(8,128)(2,1)}, bf16[2,512,256]{2,1,0:T(8,128)(2,1)S(1)}, u32[]{:S(2)}, u32[]{:S(2)}) collective-permute-start(bf16[2,512,256]{2,1,0:T(8,128)(2,1)} %collective-permute-done.11), channel_id=1, source_target_pairs={{0,8},{8,16},{16,24},{24,28},{28,20},{20,12},{12,4},{4,0},{2,6},{1... | collective-permute-start | bytes 1572872 | tf_op jit(solution)/shard_map/ppermute | solution.py:366
  38.7 4.1 %collective-permute-done.2 = bf16[2,512,256]{2,1,0:T(8,128)(2,1)S(1)} collective-permute-done((bf16[2,512,256]{2,1,0:T(8,128)(2,1)S(1)}, bf16[2,512,256]{2,1,0:T(8,128)(2,1)S(1)}, u32[]{:S(2)}, u32[]{:S(2)}) %collective-permute-start.2) | collective-permute-done | bytes 524320 | tf_op jit(solution)/shard_map/ppermute | solution.py:366
  42.8 1.4 %collective-permute-start.4 = (bf16[2,512,256]{2,1,0:T(8,128)(2,1)S(1)}, bf16[2,512,256]{2,1,0:T(8,128)(2,1)S(1)}, u32[]{:S(2)}, u32[]{:S(2)}) collective-permute-start(bf16[2,512,256]{2,1,0:T(8,128)(2,1)S(1)} %collective-permute-done.2), channel_id=1, source_target_pairs={{0,8},{8,16},{16,24},{24,28},{28,20},{20,12},{12,4},{4,0},{2,6},{1... | collective-permute-start | bytes 1572872 | tf_op jit(solution)/shard_map/ppermute | solution.py:366
  44.2 1.6 %collective-permute-start.12 = (bf16[2,512,256]{2,1,0:T(8,128)(2,1)}, bf16[2,512,256]{2,1,0:T(8,128)(2,1)}, u32[]{:S(2)}, u32[]{:S(2)}) collective-permute-start(bf16[2,512,256]{2,1,0:T(8,128)(2,1)} %collective-permute-done.11), channel_id=1, source_target_pairs={{0,2},{2,0},{8,10},{10,8},{16,18},{18,16},{24,26},{26,24},{28,30},... | collective-permute-start | bytes 1572872 | tf_op jit(solution)/shard_map/ppermute | solution.py:368
  45.8 1.3 %fusion.slot_ref = s32[16]{0:T(128)} fusion(s32[16,16]{1,0:T(8,128)} %constant.45.clone, s32[]{:T(128)S(6)} %select_n.6), kind=kLoop, calls=%fused_computation.26 | loop fusion | bytes 132 | tf_op jit(solution)/shard_map/squeeze | solution.py:436
  47.1 0.7 copy-done.5
  47.7 0.7 copy.9.pairs_ref
  48.4 0.8 constant_dynamic-update-slice_fusion.12
  49.2 0.0 collective-permute-start.3
  49.2 0.8 constant_dynamic-update-slice_fusion.21
  50.1 0.0 collective-permute-done.13
  50.1 0.2 collective-permute-start.15
  50.3 1.9 %constant_dynamic-update-slice_fusion.11 = bf16[16,512,256]{2,1,0:T(8,128)(2,1)} fusion(bf16[16,512,256]{2,1,0:T(8,128)(2,1)} %constant_dynamic-update-slice_fusion.12, bf16[2,512,256]{2,1,0:T(8,128)(2,1)} %collective-permute-done.11), kind=kLoop, calls=%fused_computation.12 | loop fusion | bytes 1048576 | tf_op jit(solution)/shard_map/dynamic_update_slice | solution.py:358
  52.2 1.9 %collective-permute-start.14 = (bf16[2,512,256]{2,1,0:T(8,128)(2,1)S(1)}, bf16[2,512,256]{2,1,0:T(8,128)(2,1)S(1)}, u32[]{:S(2)}, u32[]{:S(2)}) collective-permute-start(bf16[2,512,256]{2,1,0:T(8,128)(2,1)S(1)} %collective-permute-done.13), channel_id=1, source_target_pairs={{0,2},{2,0},{8,10},{10,8},{16,18},{18,16},{24,26},{26,24},{28,30},... | collective-permute-start | bytes 1572872 | tf_op jit(solution)/shard_map/ppermute | solution.py:368
  54.0 0.0 collective-permute-done.4
  54.0 1.4 %collective-permute-start.6 = (bf16[2,512,256]{2,1,0:T(8,128)(2,1)S(1)}, bf16[2,512,256]{2,1,0:T(8,128)(2,1)S(1)}, u32[]{:S(2)}, u32[]{:S(2)}) collective-permute-start(bf16[2,512,256]{2,1,0:T(8,128)(2,1)S(1)} %collective-permute-done.4), channel_id=1, source_target_pairs={{0,8},{8,16},{16,24},{24,28},{28,20},{20,12},{12,4},{4,0},{2,6},{1... | collective-permute-start | bytes 1572872 | tf_op jit(solution)/shard_map/ppermute | solution.py:366
  55.4 0.8 constant_dynamic-update-slice_fusion.20
  56.3 0.0 collective-permute-done.12
  56.3 1.6 %collective-permute-start.5 = (bf16[2,512,256]{2,1,0:T(8,128)(2,1)S(1)}, bf16[2,512,256]{2,1,0:T(8,128)(2,1)S(1)}, u32[]{:S(2)}, u32[]{:S(2)}) collective-permute-start(bf16[2,512,256]{2,1,0:T(8,128)(2,1)S(1)} %collective-permute-done.4), channel_id=1, source_target_pairs={{0,2},{2,0},{8,10},{10,8},{16,18},{18,16},{24,26},{26,24},{28,30},... | collective-permute-start | bytes 1572872 | tf_op jit(solution)/shard_map/ppermute | solution.py:368
  57.8 1.9 %constant_dynamic-update-slice_fusion.10 = bf16[16,512,256]{2,1,0:T(8,128)(2,1)} fusion(bf16[16,512,256]{2,1,0:T(8,128)(2,1)} %constant_dynamic-update-slice_fusion.11, bf16[2,512,256]{2,1,0:T(8,128)(2,1)} %collective-permute-done.12), kind=kLoop, calls=%fused_computation.11 | loop fusion | bytes 1048576 | tf_op jit(solution)/shard_map/dynamic_update_slice | solution.py:358
  59.7 0.8 constant_dynamic-update-slice_fusion.9
  60.6 0.0 collective-permute-done.3
  60.6 0.8 constant_dynamic-update-slice_fusion.19
  61.4 0.0 collective-permute-start.16
  61.4 0.8 constant_dynamic-update-slice_fusion.18
  62.3 0.9 collective-permute-start.17
  63.2 2.1 %collective-permute-done.6 = bf16[2,512,256]{2,1,0:T(8,128)(2,1)S(1)} collective-permute-done((bf16[2,512,256]{2,1,0:T(8,128)(2,1)S(1)}, bf16[2,512,256]{2,1,0:T(8,128)(2,1)S(1)}, u32[]{:S(2)}, u32[]{:S(2)}) %collective-permute-start.6) | collective-permute-done | bytes 524320 | tf_op jit(solution)/shard_map/ppermute | solution.py:366
  65.3 1.4 %collective-permute-start.8 = (bf16[1,512,256]{2,1,0:T(8,128)(2,1)S(1)}, bf16[1,512,256]{2,1,0:T(8,128)(2,1)S(1)}, u32[]{:S(2)}, u32[]{:S(2)}) collective-permute-start(bf16[1,512,256]{2,1,0:T(8,128)(2,1)S(1)} %slice.10), channel_id=1, source_target_pairs={{0,8},{8,16},{16,24},{24,28},{28,20},{20,12},{12,4},{4,0},{2,6},{1... | collective-permute-start | bytes 786440 | tf_op jit(solution)/shard_map/ppermute | solution.py:366
  66.7 0.0 collective-permute-done.14
  66.7 1.6 %collective-permute-start.7 = (bf16[2,512,256]{2,1,0:T(8,128)(2,1)S(1)}, bf16[2,512,256]{2,1,0:T(8,128)(2,1)S(1)}, u32[]{:S(2)}, u32[]{:S(2)}) collective-permute-start(bf16[2,512,256]{2,1,0:T(8,128)(2,1)S(1)} %collective-permute-done.6), channel_id=1, source_target_pairs={{0,2},{2,0},{8,10},{10,8},{16,18},{18,16},{24,26},{26,24},{28,30},... | collective-permute-start | bytes 1572872 | tf_op jit(solution)/shard_map/ppermute | solution.py:368
  68.3 0.8 constant_dynamic-update-slice_fusion.8
  69.2 0.8 constant_dynamic-update-slice_fusion.7
  70.0 0.0 collective-permute-done.5
  70.0 0.8 constant_dynamic-update-slice_fusion.17
  70.8 0.8 constant_dynamic-update-slice_fusion.16
  71.7 0.0 collective-permute-start.18
  71.7 0.0 collective-permute-done.8
  71.7 1.2 %collective-permute-start.9 = (bf16[1,512,256]{2,1,0:T(8,128)(2,1)S(1)}, bf16[1,512,256]{2,1,0:T(8,128)(2,1)S(1)}, u32[]{:S(2)}, u32[]{:S(2)}) collective-permute-start(bf16[1,512,256]{2,1,0:T(8,128)(2,1)S(1)} %collective-permute-done.8), channel_id=1, source_target_pairs={{0,2},{2,0},{8,10},{10,8},{16,18},{18,16},{24,26},{26,24},{28,30},... | collective-permute-start | bytes 786440 | tf_op jit(solution)/shard_map/ppermute | solution.py:368
  72.9 0.0 collective-permute-done.16
  72.9 0.8 constant_dynamic-update-slice_fusion.6
  73.7 0.0 collective-permute-done.7
  73.7 0.8 constant_dynamic-update-slice_fusion.15
  74.5 0.8 constant_dynamic-update-slice_fusion.5
  75.3 0.7 constant_dynamic-update-slice_fusion.14
  76.0 0.0 collective-permute-done.18
  76.0 0.8 constant_dynamic-update-slice_fusion.4.refs_1_
  76.8 0.7 constant_dynamic-update-slice_fusion.13.refs_0_
  77.5 24.9 %cross_spectra.1 = bf16[8,32,32,16,128]{4,3,2,1,0:T(8,128)(2,1)} custom-call(s32[8,2]{1,0:T(8,128)} %copy.9.pairs_ref, s32[16]{0:T(128)} %fusion.slot_ref, bf16[16,512,256]{2,1,0:T(8,128)(2,1)} %constant_dynamic-update-slice_fusion.13.refs_0_, bf16[16,512,256]{2,1,0:T(8,128)(2,1)} %constant_dynamic-update-slice_fusion.4.refs_1_), custom_call_target="tpu_custom_call" | custom-call | tf_op jit(solution)/shard_map/cross_spectra/pallas_call | solution.py:317
  (21 shorter events, 0.1 us)
Async XLA Ops:
  0.0 1.6 %copy-start = (bf16[64,4,4096]{2,1,0:T(4,128)(2,1)S(1)}, bf16[64,4,4096]{2,1,0:T(4,128)(2,1)}, u32[]{:S(2)}) copy-start(bf16[64,4,4096]{2,1,0:T(4,128)(2,1)} %param.8) | copy-start | bytes 6291460
  0.0 3.3 %copy-start.2 = (bf16[384,256]{1,0:T(8,128)(2,1)S(1)}, bf16[384,256]{1,0:T(8,128)(2,1)}, u32[]{:S(2)}) copy-start(bf16[384,256]{1,0:T(8,128)(2,1)} %constant.43.clone.inner_ref) | copy-start | bytes 589828
  0.0 3.4 %copy-start.4 = (bf16[128,128]{1,0:T(8,128)(2,1)S(1)}, bf16[128,128]{1,0:T(8,128)(2,1)}, u32[]{:S(2)}) copy-start(bf16[128,128]{1,0:T(8,128)(2,1)} %constant.42.clone.order_ref) | copy-start | bytes 98308
  0.0 19.8 %copy-start.3 = (bf16[128,256]{1,0:T(8,128)(2,1)S(1)}, bf16[128,256]{1,0:T(8,128)(2,1)}, u32[]{:S(2)}) copy-start(bf16[128,256]{1,0:T(8,128)(2,1)} %constant.44.clone.first_ref) | copy-start | bytes 196612
  5.3 14.5 %collective-permute-start = (bf16[128,2176]{1,0:T(8,128)(2,1)S(1)}, bf16[128,2176]{1,0:T(8,128)(2,1)S(1)}, u32[]{:S(2)}, u32[]{:S(2)}) collective-permute-start(bf16[128,2176]{1,0:T(8,128)(2,1)S(1)} %decimate.1.own_ref), channel_id=1, source_target_pairs={{0,1},{1,0},{2,3},{3,2},{4,5},{5,4},{6,7},{7,6},{8,9},{9,8},{10,11... | collective-permute-start | bytes 1671176 | tf_op jit(solution)/shard_map/ppermute | solution.py:412
  26.3 2.5 %collective-permute-start.10 = (bf16[1,512,256]{2,1,0:T(8,128)(2,1)S(1)}, bf16[1,512,256]{2,1,0:T(8,128)(2,1)S(1)}, u32[]{:S(2)}, u32[]{:S(2)}) collective-permute-start(bf16[1,512,256]{2,1,0:T(8,128)(2,1)S(1)} %get-tuple-element.8), channel_id=1, source_target_pairs={{0,2},{2,0},{8,10},{10,8},{16,18},{18,16},{24,26},{26,24},{28,30},... | collective-permute-start | bytes 786440 | tf_op jit(solution)/shard_map/ppermute | solution.py:360
  27.6 2.7 %collective-permute-start.1 = (bf16[1,512,256]{2,1,0:T(8,128)(2,1)S(1)}, bf16[1,512,256]{2,1,0:T(8,128)(2,1)S(1)}, u32[]{:S(2)}, u32[]{:S(2)}) collective-permute-start(bf16[1,512,256]{2,1,0:T(8,128)(2,1)S(1)} %get-tuple-element.7), channel_id=1, source_target_pairs={{0,2},{2,0},{8,10},{10,8},{16,18},{18,16},{24,26},{26,24},{28,30},... | collective-permute-start | bytes 786440 | tf_op jit(solution)/shard_map/ppermute | solution.py:360
  28.7 8.5 %collective-permute-start.11 = (bf16[2,512,256]{2,1,0:T(8,128)(2,1)S(1)}, bf16[2,512,256]{2,1,0:T(8,128)(2,1)}, u32[]{:S(2)}, u32[]{:S(2)}) collective-permute-start(bf16[2,512,256]{2,1,0:T(8,128)(2,1)S(1)} %constant_dynamic-update-slice_fusion.2), channel_id=1, source_target_pairs={{0,8},{8,16},{16,24},{24,28},{28,20},{20,12},{12,4},{4,0},{2,6},{1... | collective-permute-start | bytes 1572872 | tf_op jit(solution)/shard_map/ppermute | solution.py:366
  30.3 12.5 %collective-permute-start.2 = (bf16[2,512,256]{2,1,0:T(8,128)(2,1)S(1)}, bf16[2,512,256]{2,1,0:T(8,128)(2,1)S(1)}, u32[]{:S(2)}, u32[]{:S(2)}) collective-permute-start(bf16[2,512,256]{2,1,0:T(8,128)(2,1)S(1)} %constant_dynamic-update-slice_fusion), channel_id=1, source_target_pairs={{0,8},{8,16},{16,24},{24,28},{28,20},{20,12},{12,4},{4,0},{2,6},{1... | collective-permute-start | bytes 1572872 | tf_op jit(solution)/shard_map/ppermute | solution.py:366
  37.3 12.8 %collective-permute-start.13 = (bf16[2,512,256]{2,1,0:T(8,128)(2,1)}, bf16[2,512,256]{2,1,0:T(8,128)(2,1)S(1)}, u32[]{:S(2)}, u32[]{:S(2)}) collective-permute-start(bf16[2,512,256]{2,1,0:T(8,128)(2,1)} %collective-permute-done.11), channel_id=1, source_target_pairs={{0,8},{8,16},{16,24},{24,28},{28,20},{20,12},{12,4},{4,0},{2,6},{1... | collective-permute-start | bytes 1572872 | tf_op jit(solution)/shard_map/ppermute | solution.py:366
  42.8 11.2 %collective-permute-start.4 = (bf16[2,512,256]{2,1,0:T(8,128)(2,1)S(1)}, bf16[2,512,256]{2,1,0:T(8,128)(2,1)S(1)}, u32[]{:S(2)}, u32[]{:S(2)}) collective-permute-start(bf16[2,512,256]{2,1,0:T(8,128)(2,1)S(1)} %collective-permute-done.2), channel_id=1, source_target_pairs={{0,8},{8,16},{16,24},{24,28},{28,20},{20,12},{12,4},{4,0},{2,6},{1... | collective-permute-start | bytes 1572872 | tf_op jit(solution)/shard_map/ppermute | solution.py:366
  44.2 12.1 %collective-permute-start.12 = (bf16[2,512,256]{2,1,0:T(8,128)(2,1)}, bf16[2,512,256]{2,1,0:T(8,128)(2,1)}, u32[]{:S(2)}, u32[]{:S(2)}) collective-permute-start(bf16[2,512,256]{2,1,0:T(8,128)(2,1)} %collective-permute-done.11), channel_id=1, source_target_pairs={{0,2},{2,0},{8,10},{10,8},{16,18},{18,16},{24,26},{26,24},{28,30},... | collective-permute-start | bytes 1572872 | tf_op jit(solution)/shard_map/ppermute | solution.py:368
  47.1 0.7 copy-start.5
  49.2 11.3 %collective-permute-start.3 = (bf16[2,512,256]{2,1,0:T(8,128)(2,1)S(1)}, bf16[2,512,256]{2,1,0:T(8,128)(2,1)S(1)}, u32[]{:S(2)}, u32[]{:S(2)}) collective-permute-start(bf16[2,512,256]{2,1,0:T(8,128)(2,1)S(1)} %collective-permute-done.2), channel_id=1, source_target_pairs={{0,2},{2,0},{8,10},{10,8},{16,18},{18,16},{24,26},{26,24},{28,30},... | collective-permute-start | bytes 1572872 | tf_op jit(solution)/shard_map/ppermute | solution.py:368
  50.1 11.3 %collective-permute-start.15 = (bf16[2,512,256]{2,1,0:T(8,128)(2,1)S(1)}, bf16[2,512,256]{2,1,0:T(8,128)(2,1)S(1)}, u32[]{:S(2)}, u32[]{:S(2)}) collective-permute-start(bf16[2,512,256]{2,1,0:T(8,128)(2,1)S(1)} %collective-permute-done.13), channel_id=1, source_target_pairs={{0,8},{8,16},{16,24},{24,28},{28,20},{20,12},{12,4},{4,0},{2,6},{1... | collective-permute-start | bytes 1572872 | tf_op jit(solution)/shard_map/ppermute | solution.py:366
  52.2 14.6 %collective-permute-start.14 = (bf16[2,512,256]{2,1,0:T(8,128)(2,1)S(1)}, bf16[2,512,256]{2,1,0:T(8,128)(2,1)S(1)}, u32[]{:S(2)}, u32[]{:S(2)}) collective-permute-start(bf16[2,512,256]{2,1,0:T(8,128)(2,1)S(1)} %collective-permute-done.13), channel_id=1, source_target_pairs={{0,2},{2,0},{8,10},{10,8},{16,18},{18,16},{24,26},{26,24},{28,30},... | collective-permute-start | bytes 1572872 | tf_op jit(solution)/shard_map/ppermute | solution.py:368
  54.0 11.2 %collective-permute-start.6 = (bf16[2,512,256]{2,1,0:T(8,128)(2,1)S(1)}, bf16[2,512,256]{2,1,0:T(8,128)(2,1)S(1)}, u32[]{:S(2)}, u32[]{:S(2)}) collective-permute-start(bf16[2,512,256]{2,1,0:T(8,128)(2,1)S(1)} %collective-permute-done.4), channel_id=1, source_target_pairs={{0,8},{8,16},{16,24},{24,28},{28,20},{20,12},{12,4},{4,0},{2,6},{1... | collective-permute-start | bytes 1572872 | tf_op jit(solution)/shard_map/ppermute | solution.py:366
  56.3 13.7 %collective-permute-start.5 = (bf16[2,512,256]{2,1,0:T(8,128)(2,1)S(1)}, bf16[2,512,256]{2,1,0:T(8,128)(2,1)S(1)}, u32[]{:S(2)}, u32[]{:S(2)}) collective-permute-start(bf16[2,512,256]{2,1,0:T(8,128)(2,1)S(1)} %collective-permute-done.4), channel_id=1, source_target_pairs={{0,2},{2,0},{8,10},{10,8},{16,18},{18,16},{24,26},{26,24},{28,30},... | collective-permute-start | bytes 1572872 | tf_op jit(solution)/shard_map/ppermute | solution.py:368
  61.4 11.5 %collective-permute-start.16 = (bf16[2,512,256]{2,1,0:T(8,128)(2,1)S(1)}, bf16[2,512,256]{2,1,0:T(8,128)(2,1)S(1)}, u32[]{:S(2)}, u32[]{:S(2)}) collective-permute-start(bf16[2,512,256]{2,1,0:T(8,128)(2,1)S(1)} %collective-permute-done.15), channel_id=1, source_target_pairs={{0,2},{2,0},{8,10},{10,8},{16,18},{18,16},{24,26},{26,24},{28,30},... | collective-permute-start | bytes 1572872 | tf_op jit(solution)/shard_map/ppermute | solution.py:368
  62.3 9.4 %collective-permute-start.17 = (bf16[1,512,256]{2,1,0:T(8,128)(2,1)S(1)}, bf16[1,512,256]{2,1,0:T(8,128)(2,1)S(1)}, u32[]{:S(2)}, u32[]{:S(2)}) collective-permute-start(bf16[1,512,256]{2,1,0:T(8,128)(2,1)S(1)} %slice.11), channel_id=1, source_target_pairs={{0,8},{8,16},{16,24},{24,28},{28,20},{20,12},{12,4},{4,0},{2,6},{1... | collective-permute-start | bytes 786440 | tf_op jit(solution)/shard_map/ppermute | solution.py:366
  65.3 6.4 %collective-permute-start.8 = (bf16[1,512,256]{2,1,0:T(8,128)(2,1)S(1)}, bf16[1,512,256]{2,1,0:T(8,128)(2,1)S(1)}, u32[]{:S(2)}, u32[]{:S(2)}) collective-permute-start(bf16[1,512,256]{2,1,0:T(8,128)(2,1)S(1)} %slice.10), channel_id=1, source_target_pairs={{0,8},{8,16},{16,24},{24,28},{28,20},{20,12},{12,4},{4,0},{2,6},{1... | collective-permute-start | bytes 786440 | tf_op jit(solution)/shard_map/ppermute | solution.py:366
  66.7 7.0 %collective-permute-start.7 = (bf16[2,512,256]{2,1,0:T(8,128)(2,1)S(1)}, bf16[2,512,256]{2,1,0:T(8,128)(2,1)S(1)}, u32[]{:S(2)}, u32[]{:S(2)}) collective-permute-start(bf16[2,512,256]{2,1,0:T(8,128)(2,1)S(1)} %collective-permute-done.6), channel_id=1, source_target_pairs={{0,2},{2,0},{8,10},{10,8},{16,18},{18,16},{24,26},{26,24},{28,30},... | collective-permute-start | bytes 1572872 | tf_op jit(solution)/shard_map/ppermute | solution.py:368
  71.7 4.4 %collective-permute-start.18 = (bf16[1,512,256]{2,1,0:T(8,128)(2,1)S(1)}, bf16[1,512,256]{2,1,0:T(8,128)(2,1)S(1)}, u32[]{:S(2)}, u32[]{:S(2)}) collective-permute-start(bf16[1,512,256]{2,1,0:T(8,128)(2,1)S(1)} %collective-permute-done.17), channel_id=1, source_target_pairs={{0,2},{2,0},{8,10},{10,8},{16,18},{18,16},{24,26},{26,24},{28,30},... | collective-permute-start | bytes 786440 | tf_op jit(solution)/shard_map/ppermute | solution.py:368
  71.7 5.1 %collective-permute-start.9 = (bf16[1,512,256]{2,1,0:T(8,128)(2,1)S(1)}, bf16[1,512,256]{2,1,0:T(8,128)(2,1)S(1)}, u32[]{:S(2)}, u32[]{:S(2)}) collective-permute-start(bf16[1,512,256]{2,1,0:T(8,128)(2,1)S(1)} %collective-permute-done.8), channel_id=1, source_target_pairs={{0,2},{2,0},{8,10},{10,8},{16,18},{18,16},{24,26},{26,24},{28,30},... | collective-permute-start | bytes 786440 | tf_op jit(solution)/shard_map/ppermute | solution.py:368
  77.5 24.9 %copy-start.1 = (bf16[64,4,4096]{2,1,0:T(4,128)(2,1)S(1)}, bf16[64,4,4096]{2,1,0:T(4,128)(2,1)}, u32[]{:S(2)}) copy-start(bf16[64,4,4096]{2,1,0:T(4,128)(2,1)} %param.8) | copy-start | bytes 6291460
where the time goes:
time: 103 us; the launch traced here: 102 us
  Pallas kernels  33.3 us (32%)
  waiting for transfers between devices  25.4 us (25%)
  local copies, waits for them, and re-layouts  21.9 us (21%)
  starting transfers between devices  20.9 us (20%)
    pallas_call x1, Pallas kernels, cross_spectra(): pl.pallas_call(cross_kernel, in_specs=[smem, smem] + [hbm] * len(gathered...  24.9 us
    dynamic_update_slice x18, local copies, waits for them, and re-layouts, put(): gathered[k] = lax.dynamic_update_slice(gathered[k], piece, (slot, 0, 0))  16.7 us
    ppermute x1, waiting for transfers between devices, body(): other = lax.ppermute(message, 'band', [(0, 1), (1, 0)])  12.4 us
    ppermute x8, waiting for transfers between devices, gather_blocks(): move(current[k][:1] if step == steps else current[k], perm=ring)  11.9 us
    ppermute x8, starting transfers between devices, gather_blocks(): move(current[k][:1] if step == steps else current[k], perm=ring)  9.49 us
    ppermute x8, starting transfers between devices, gather_blocks(): put(k, move(current[k], perm=swap), 4 * step - (1 if step == steps else 0))  7.89 us
    pallas_call x1, Pallas kernels, body(): pl.pallas_call(whiten_kernel, in_specs=[pl.BlockSpec(memory_space=pltpu.S...  6.49 us
    unnamed x15, local copies, waits for them, and re-layouts  2.17 us
  transfers between devices with their start and end apart: 19, of which 5 were waited for; matrix products, arithmetic and copies ran while one was open for 18% of the time, Pallas kernels for 0%

commit v1 on v0

--- a/solution.py
+++ b/solution.py
@@ -22,6 +22,7 @@
 TILE = (4, 32)
 PIECE = 4
 TURNS = 4
+WHITEN_BYTES = 40_000_000
 VMEM_CROSS = 56
 MIB = 2**20
 
@@ -80,13 +81,16 @@
     return both[:, :LANES] + both[:, LANES:]
 
 
-def decimate_kernel(order_ref, raw_ref, inner_ref, out_ref):
+def decimate_kernel(order_ref, raw_ref, inner_ref, *out_refs):
     rows, samples = raw_ref.shape
     order = order_ref[...]
 
     def put(first_lane, value):
-        moved = jnp.dot(order, value, preferred_element_type=jnp.float32)
-        out_ref[:, first_lane : first_lane + value.shape[1]] = moved.astype(jnp.bfloat16)
+        moved = jnp.dot(order, value, preferred_element_type=jnp.float32).astype(jnp.bfloat16)
+        first = 0
+        for out_ref in out_refs:
+            out_ref[:, first_lane : first_lane + value.shape[1]] = moved[first : first + out_ref.shape[0]]
+            first += out_ref.shape[0]
 
     blocks = samples // (2 * LANES)
     for block in range(0, blocks, 2):
@@ -108,9 +112,9 @@
     put(blocks * LANES, edge)
 
 
-def whiten_kernel(band_ref, own_ref, other_ref, first_ref, table_ref, *refs):
-    chunk_refs = refs[: len(CHUNKS)]
-    halves_ref, spectra_ref, spread_ref, tiles_ref, table_sem = refs[len(CHUNKS) :]
+def whiten_kernel(
+    band_ref, own_ref, other_ref, first_ref, table_ref, out_ref, halves_ref, spectra_ref, spread_ref, tiles_ref, table_sem
+):
     tiles = tiles_ref.shape[0]
 
     def tile_copy(tile):
@@ -182,12 +186,8 @@
                 for c in range(0, channels, 8):
                     base = (c * WIN + w) * 8 + 2 * (t % 4) + part
                     spread_ref[t // 4, pl.ds(base, 8, stride=8 * WIN), :] = value[c : c + 8]
-    first = 0
-    for chunk_ref in chunk_refs:
-        size = chunk_ref.shape[1]
-        sides = [spread_ref[k, first : first + size] for k in range(count // 4)]
-        chunk_ref[0] = jnp.concatenate(sides, axis=1).astype(jnp.bfloat16)
-        first += size
+    sides = [spread_ref[k] for k in range(count // 4)]
+    out_ref[0] = jnp.concatenate(sides, axis=1).astype(jnp.bfloat16)
 
 
 def cross_kernel(pairs_ref, slot_ref, *refs):
@@ -352,20 +352,24 @@
 def gather_blocks(chunks, swap, ring):
     move = functools.partial(lax.ppermute, axis_name="chan")
     count = len(ring)
+    current = [jnp.concatenate([own, move(own, perm=swap)], axis=0) for own in chunks]
     gathered = [reserve((count,) + own.shape[1:]) for own in chunks]
 
-    def put(k, piece, slot):
+    def put(k, pieces, slot):
+        piece = jnp.concatenate(pieces, axis=0) if len(pieces) > 1 else pieces[0]
         gathered[k] = lax.dynamic_update_slice(gathered[k], piece, (slot, 0, 0))
 
-    current = [jnp.concatenate([own, move(own, perm=swap)], axis=0) for own in chunks]
-    for k, piece in enumerate(current):
-        put(k, piece, 0)
     steps = count // 4
+    waiting = [([piece], 0) for piece in current]
     for step in range(1, steps + 1):
-        for k in range(len(chunks)):
+        for k in range(len(current)):
             current[k] = move(current[k][:1] if step == steps else current[k], perm=ring)
-            put(k, current[k], 4 * step - 2)
-            put(k, move(current[k], perm=swap), 4 * step - (1 if step == steps else 0))
+            put(k, *waiting[k])
+            waiting[k] = ([current[k], move(current[k], perm=swap)], 4 * step - 2)
+            if step < steps:
+                current[k], gathered[k] = lax.optimization_barrier((current[k], gathered[k]))
+    for k, last in enumerate(waiting):
+        put(k, *last)
     return gathered
 
 
@@ -398,36 +402,44 @@
     inner, first = fir_matrices()
     table = jnp.asarray(trig_tables(2, bins_dev, length))
     order = np.zeros((rows, rows), jnp.bfloat16)
-    for window in range(WIN):
-        for channel in range(channels):
-            order[window * channels + channel, channel * WIN + window] = 1
-
-    picked = raw.at[selection].get(mode="promise_in_bounds").reshape(rows, samples)
-    message = pl.pallas_call(
+    first_channel = 0
+    for size in CHUNKS:
+        for window in range(WIN):
+            for channel in range(size):
+                row = first_channel * WIN + window * size + channel
+                order[row, (first_channel + channel) * WIN + window] = 1
+        first_channel += size
+
+    picked = raw.at[selection].get(mode="promise_in_bounds", wrap_negative_indices=False).reshape(rows, samples)
+    vmem = pl.BlockSpec(memory_space=pltpu.VMEM)
+    messages = pl.pallas_call(
         decimate_kernel,
-        out_shape=jax.ShapeDtypeStruct((rows, length + LANES), jnp.bfloat16),
+        out_shape=[jax.ShapeDtypeStruct((size * WIN, length + LANES), jnp.bfloat16) for size in CHUNKS],
         compiler_params=pltpu.CompilerParams(vmem_limit_bytes=24 * MIB),
         name="decimate",
     )(jnp.asarray(order), picked, jnp.asarray(inner))
-    other = lax.ppermute(message, "band", [(0, 1), (1, 0)])
-
-    vmem = pl.BlockSpec(memory_space=pltpu.VMEM)
-    chunk_shapes = [(1, size * WIN * 8, tiles // 4 * LANES) for size in CHUNKS]
-    chunks = pl.pallas_call(
-        whiten_kernel,
-        in_specs=[pl.BlockSpec(memory_space=pltpu.SMEM), vmem, vmem, vmem, pl.BlockSpec(memory_space=pltpu.HBM)],
-        out_specs=[vmem] * len(CHUNKS),
-        scratch_shapes=[
-            pltpu.VMEM((2 * rows, length), jnp.bfloat16),
-            pltpu.VMEM((tiles + 1, rows, 2 * LANES), jnp.float32),
-            pltpu.VMEM((tiles // 4, rows * 8, LANES), jnp.float32),
-            pltpu.VMEM(table.shape[1:], jnp.bfloat16),
-            pltpu.SemaphoreType.DMA((tiles + 1,)),
-        ],
-        out_shape=[jax.ShapeDtypeStruct(shape, jnp.bfloat16) for shape in chunk_shapes],
-        compiler_params=pltpu.CompilerParams(vmem_limit_bytes=50 * MIB),
-        name="whiten",
-    )(band, message, other, jnp.asarray(first), table)
+    others = [lax.ppermute(message, "band", [(0, 1), (1, 0)]) for message in messages]
+
+    def whiten(message, other):
+        count = message.shape[0]
+        return pl.pallas_call(
+            whiten_kernel,
+            in_specs=[pl.BlockSpec(memory_space=pltpu.SMEM), vmem, vmem, vmem, pl.BlockSpec(memory_space=pltpu.HBM)],
+            out_specs=vmem,
+            scratch_shapes=[
+                pltpu.VMEM((2 * count, length), jnp.bfloat16),
+                pltpu.VMEM((tiles + 1, count, 2 * LANES), jnp.float32),
+                pltpu.VMEM((tiles // 4, count * 8, LANES), jnp.float32),
+                pltpu.VMEM(table.shape[1:], jnp.bfloat16),
+                pltpu.SemaphoreType.DMA((tiles + 1,)),
+            ],
+            out_shape=jax.ShapeDtypeStruct((1, count * 8, tiles // 4 * LANES), jnp.bfloat16),
+            compiler_params=pltpu.CompilerParams(vmem_limit_bytes=50 * MIB),
+            cost_estimate=pl.CostEstimate(flops=0, bytes_accessed=WHITEN_BYTES, transcendentals=0),
+            name="whiten",
+        )(band, message, other, jnp.asarray(first), table)
+
+    chunks = [whiten(message, other) for message, other in zip(messages, others)]
 
     count = len(positions)
     swap = [(chip[c], chip[1 - c]) for chip in positions for c in range(2)]

time: 103 us -> 99.9 us (0.970)
  local copies, waits for them, and re-layouts: 21.9 us -> 4.51 us
  other arithmetic: 0.82 us -> 10.7 us
  starting transfers between devices: 20.9 us -> 27.2 us
  waiting for transfers between devices: 25.4 us -> 20.5 us
  Pallas kernels: 33.3 us -> 36.6 us
    dynamic_update_slice x18 -> x0, local copies, waits for them, and re-layouts: 16.7 us -> none  [put(): gathered[k] = lax.dynamic_update_slice(gathered[k], piece, (slot, 0, 0))]
    dynamic_update_slice x0 -> x10, other arithmetic: none -> 9.92 us  [put(): gathered[k] = lax.dynamic_update_slice(gathered[k], piece, (slot, 0, 0))]
    ppermute x9 -> x10, waiting for transfers between devices: 12.4 us -> 6.33 us  [the longest x2 6.31 us: body(): lax.ppermute(message, 'band', [(0, 1), (1, 0)])]
    pallas_call x2 -> x3, Pallas kernels: 8.4 us -> 11.7 us  [the longest x2 9.82 us: whiten(): pl.pallas_call(whiten_kernel, in_specs=[pl.BlockSpec(memory_space=pltpu.S...]
    ppermute x8, starting transfers between devices: 9.49 us -> 12.4 us  [gather_blocks(): move(current[k][:1] if step == steps else current[k], perm=ring)]
    ppermute x9 -> x10, starting transfers between devices: 10 us -> 12.5 us  [the longest x8 10.3 us: gather_blocks(): waiting[k] = ([current[k], move(current[k], perm=swap)], 4 * step - 2)]
    ppermute x8, waiting for transfers between devices: 11.9 us -> 14.2 us  [gather_blocks(): move(current[k][:1] if step == steps else current[k], perm=ring)]
    ppermute x2, waiting for transfers between devices: 1.06 us -> 0.01 us  [gather_blocks(): move(own, perm=swap)]
  transfers between devices with their start and end apart: 19 -> 20, of which waited for: 5 -> 7; matrix products, arithmetic and copies ran while one was open for 18% -> 11% of each run, Pallas kernels for 0% -> 10%
where the time goes in v1:
time: 99.9 us; the launch traced here: 99.7 us
  Pallas kernels  36.6 us (37%)
  starting transfers between devices  27.2 us (27%)
  waiting for transfers between devices  20.5 us (21%)
  other arithmetic  10.7 us (11%)
  local copies, waits for them, and re-layouts  4.51 us (5%)
    pallas_call x1, Pallas kernels, cross_spectra(): pl.pallas_call(cross_kernel, in_specs=[smem, smem] + [hbm] * len(gathered...  24.9 us
    ppermute x8, waiting for transfers between devices, gather_blocks(): move(current[k][:1] if step == steps else current[k], perm=ring)  14.2 us
    ppermute x8, starting transfers between devices, gather_blocks(): move(current[k][:1] if step == steps else current[k], perm=ring)  12.4 us
    ppermute x8, starting transfers between devices, gather_blocks(): waiting[k] = ([current[k], move(current[k], perm=swap)], 4 * step - 2)  10.3 us
    dynamic_update_slice x10, other arithmetic, put(): gathered[k] = lax.dynamic_update_slice(gathered[k], piece, (slot, 0, 0))  9.92 us
    pallas_call x2, Pallas kernels, whiten(): pl.pallas_call(whiten_kernel, in_specs=[pl.BlockSpec(memory_space=pltpu.S...  9.82 us
    ppermute x2, waiting for transfers between devices, body(): lax.ppermute(message, 'band', [(0, 1), (1, 0)])  6.31 us
    ppermute x2, starting transfers between devices, gather_blocks(): move(own, perm=swap)  2.34 us
  transfers between devices with their start and end apart: 20, of which 7 were waited for; matrix products, arithmetic and copies ran while one was open for 11% of the time, Pallas kernels for 10%

profile of v1, /device:TPU:1, one launch (start us, length us, event | category | flops | bytes accessed | tf_op | source)
XLA Modules:
  0.0 99.7 jit_solution(4317387617988095269)
XLA Ops:
  0.0 0.0 copy-start
  0.0 0.0 copy-start.2
  0.0 0.8 pad_clamp_fusion
  0.8 0.8 copy-done
  1.6 1.4 %gather_fusion = bf16[32,4,4096]{2,1,0:T(4,128)(2,1)S(1)} fusion(bf16[64,4,4096]{2,1,0:T(4,128)(2,1)S(1)} %copy-done, s32[1024]{0:T(1024)S(1)} %pad_clamp_fusion), kind=kCustom, calls=%fused_computation | custom fusion | bytes 2097280 | tf_op jit(solution)/shard_map/gather | solution.py:413
  3.1 0.3 reshape.13.raw_ref
  3.3 0.0 copy-done.3
  3.4 0.0 copy-done.4
  3.4 1.9 %decimate.1 = (bf16[64,2176]{1,0:T(8,128)(2,1)S(1)}, bf16[64,2176]{1,0:T(8,128)(2,1)S(1)}) custom-call(bf16[128,128]{1,0:T(8,128)(2,1)S(1)} %copy-done.4, bf16[128,4096]{1,0:T(8,128)(2,1)S(1)} %reshape.13.raw_ref, bf16[384,256]{1,0:T(8,128)(2,1)S(1)} %copy-done.3), custom_call_target="tpu_custom_call" | custom-call | tf_op jit(solution)/shard_map/decimate/pallas_call | solution.py:415
  5.3 2.1 %collective-permute-start.10 = (bf16[64,2176]{1,0:T(8,128)(2,1)S(1)}, bf16[64,2176]{1,0:T(8,128)(2,1)S(1)}, u32[]{:S(2)}, u32[]{:S(2)}) collective-permute-start(bf16[64,2176]{1,0:T(8,128)(2,1)S(1)} %get-tuple-element.26.own_ref), channel_id=1, source_target_pairs={{0,1},{1,0},{2,3},{3,2},{4,5},{5,4},{6,7},{7,6},{8,9},{9,8},{10,11... | collective-permute-start | bytes 835592 | tf_op jit(solution)/shard_map/ppermute | solution.py:421
  7.4 0.1 collective-permute-start
  7.5 6.3 %collective-permute-done.10.other_ref = bf16[64,2176]{1,0:T(8,128)(2,1)S(1)} collective-permute-done((bf16[64,2176]{1,0:T(8,128)(2,1)S(1)}, bf16[64,2176]{1,0:T(8,128)(2,1)S(1)}, u32[]{:S(2)}, u32[]{:S(2)}) %collective-permute-start.10) | collective-permute-done | bytes 278560 | tf_op jit(solution)/shard_map/ppermute | solution.py:421
  13.8 4.9 %whiten.3 = bf16[1,512,256]{2,1,0:T(8,128)(2,1)S(1)} custom-call(s32[1]{0:T(128)} %bitcast.1.band_ref, bf16[64,2176]{1,0:T(8,128)(2,1)S(1)} %get-tuple-element.26.own_ref, bf16[64,2176]{1,0:T(8,128)(2,1)S(1)} %collective-permute-done.10.other_ref, bf16[128,256]{1,0:T(8,128)(2,1)S(1)} %copy-done.2, bf16[2,9,2048,256]{3,2,1,0:T(8,128)(2,1)} %constant.30.clone.table_ref), custom_call_target="tpu_custom_call" | custom-call | bytes 40000000 | tf_op jit(solution)/shard_map/whiten/pallas_call | solution.py:425
  18.7 2.1 %collective-permute-start.11 = (bf16[1,512,256]{2,1,0:T(8,128)(2,1)S(1)}, bf16[1,512,256]{2,1,0:T(8,128)(2,1)S(1)}, u32[]{:S(2)}, u32[]{:S(2)}) collective-permute-start(bf16[1,512,256]{2,1,0:T(8,128)(2,1)S(1)} %whiten.3), channel_id=1, source_target_pairs={{0,2},{2,0},{8,10},{10,8},{16,18},{18,16},{24,26},{26,24},{28,30},... | collective-permute-start | bytes 786440 | tf_op jit(solution)/shard_map/ppermute | solution.py:355
  20.8 0.0 collective-permute-done.other_ref
  20.9 4.9 %whiten.2 = bf16[1,512,256]{2,1,0:T(8,128)(2,1)S(1)} custom-call(s32[1]{0:T(128)} %bitcast.1.band_ref, bf16[64,2176]{1,0:T(8,128)(2,1)S(1)} %get-tuple-element.19.own_ref, bf16[64,2176]{1,0:T(8,128)(2,1)S(1)} %collective-permute-done.other_ref, bf16[128,256]{1,0:T(8,128)(2,1)S(1)} %copy-done.2, bf16[2,9,2048,256]{3,2,1,0:T(8,128)(2,1)} %constant.30.clone.table_ref), custom_call_target="tpu_custom_call" | custom-call | bytes 40000000 | tf_op jit(solution)/shard_map/whiten/pallas_call | solution.py:425
  25.8 0.2 collective-permute-start.1
  26.0 0.0 collective-permute-done.11
  26.0 0.9 constant_dynamic-update-slice_fusion
  26.9 1.6 %collective-permute-start.12 = (bf16[2,512,256]{2,1,0:T(8,128)(2,1)S(1)}, bf16[2,512,256]{2,1,0:T(8,128)(2,1)S(1)}, u32[]{:S(2)}, u32[]{:S(2)}) collective-permute-start(bf16[2,512,256]{2,1,0:T(8,128)(2,1)S(1)} %get-tuple-element.34), channel_id=1, source_target_pairs={{0,8},{8,16},{16,24},{24,28},{28,20},{20,12},{12,4},{4,0},{2,6},{1... | collective-permute-start | bytes 1572872 | tf_op jit(solution)/shard_map/ppermute | solution.py:366
  28.5 0.0 collective-permute-done.1
  28.5 0.9 constant_dynamic-update-slice_fusion.1
  29.4 1.3 %collective-permute-start.2 = (bf16[2,512,256]{2,1,0:T(8,128)(2,1)S(1)}, bf16[2,512,256]{2,1,0:T(8,128)(2,1)S(1)}, u32[]{:S(2)}, u32[]{:S(2)}) collective-permute-start(bf16[2,512,256]{2,1,0:T(8,128)(2,1)S(1)} %get-tuple-element.36), channel_id=1, source_target_pairs={{0,8},{8,16},{16,24},{24,28},{28,20},{20,12},{12,4},{4,0},{2,6},{1... | collective-permute-start | bytes 1572872 | tf_op jit(solution)/shard_map/ppermute | solution.py:366
  30.7 4.8 %collective-permute-done.12 = bf16[2,512,256]{2,1,0:T(8,128)(2,1)S(1)} collective-permute-done((bf16[2,512,256]{2,1,0:T(8,128)(2,1)S(1)}, bf16[2,512,256]{2,1,0:T(8,128)(2,1)S(1)}, u32[]{:S(2)}, u32[]{:S(2)}) %collective-permute-start.12) | collective-permute-done | bytes 524320 | tf_op jit(solution)/shard_map/ppermute | solution.py:366
  35.5 1.0 collective-permute-start.14
  36.5 1.7 %collective-permute-start.13 = (bf16[2,512,256]{2,1,0:T(8,128)(2,1)S(1)}, bf16[2,512,256]{2,1,0:T(8,128)(2,1)S(1)}, u32[]{:S(2)}, u32[]{:S(2)}) collective-permute-start(bf16[2,512,256]{2,1,0:T(8,128)(2,1)S(1)} %collective-permute-done.12), channel_id=1, source_target_pairs={{0,8},{8,16},{16,24},{24,28},{28,20},{20,12},{12,4},{4,0},{2,6},{1... | collective-permute-start | bytes 1572872 | tf_op jit(solution)/shard_map/ppermute | solution.py:366
  38.2 2.9 %collective-permute-done.2 = bf16[2,512,256]{2,1,0:T(8,128)(2,1)S(1)} collective-permute-done((bf16[2,512,256]{2,1,0:T(8,128)(2,1)S(1)}, bf16[2,512,256]{2,1,0:T(8,128)(2,1)S(1)}, u32[]{:S(2)}, u32[]{:S(2)}) %collective-permute-start.2) | collective-permute-done | bytes 524320 | tf_op jit(solution)/shard_map/ppermute | solution.py:366
  41.1 1.4 %collective-permute-start.3 = (bf16[2,512,256]{2,1,0:T(8,128)(2,1)S(1)}, bf16[2,512,256]{2,1,0:T(8,128)(2,1)S(1)}, u32[]{:S(2)}, u32[]{:S(2)}) collective-permute-start(bf16[2,512,256]{2,1,0:T(8,128)(2,1)S(1)} %collective-permute-done.2), channel_id=1, source_target_pairs={{0,8},{8,16},{16,24},{24,28},{28,20},{20,12},{12,4},{4,0},{2,6},{1... | collective-permute-start | bytes 1572872 | tf_op jit(solution)/shard_map/ppermute | solution.py:366
  42.5 1.7 %collective-permute-start.4 = (bf16[2,512,256]{2,1,0:T(8,128)(2,1)S(1)}, bf16[2,512,256]{2,1,0:T(8,128)(2,1)S(1)}, u32[]{:S(2)}, u32[]{:S(2)}) collective-permute-start(bf16[2,512,256]{2,1,0:T(8,128)(2,1)S(1)} %collective-permute-done.2), channel_id=1, source_target_pairs={{0,2},{2,0},{8,10},{10,8},{16,18},{18,16},{24,26},{26,24},{28,30},... | collective-permute-start | bytes 1572872 | tf_op jit(solution)/shard_map/ppermute | solution.py:368
  44.2 0.0 collective-permute-done.14
  44.2 1.1 %maximum_dynamic-update-slice_fusion.3 = bf16[16,512,256]{2,1,0:T(8,128)(2,1)} fusion(bf16[16,512,256]{2,1,0:T(8,128)(2,1)} %get-tuple-element.28, bf16[2,512,256]{2,1,0:T(8,128)(2,1)S(1)} %collective-permute-done.14, bf16[2,512,256]{2,1,0:T(8,128)(2,1)S(1)} %collective-permute-done.12), kind=kLoop, calls=%fused_computation.4 | loop fusion | flops 2097152 | bytes 2097152 | tf_op jit(solution)/shard_map/dynamic_update_slice | solution.py:360
  45.3 1.5 %collective-permute-done.13 = bf16[2,512,256]{2,1,0:T(8,128)(2,1)S(1)} collective-permute-done((bf16[2,512,256]{2,1,0:T(8,128)(2,1)S(1)}, bf16[2,512,256]{2,1,0:T(8,128)(2,1)S(1)}, u32[]{:S(2)}, u32[]{:S(2)}) %collective-permute-start.13) | collective-permute-done | bytes 524320 | tf_op jit(solution)/shard_map/ppermute | solution.py:366
  46.7 1.4 %collective-permute-start.15 = (bf16[2,512,256]{2,1,0:T(8,128)(2,1)S(1)}, bf16[2,512,256]{2,1,0:T(8,128)(2,1)S(1)}, u32[]{:S(2)}, u32[]{:S(2)}) collective-permute-start(bf16[2,512,256]{2,1,0:T(8,128)(2,1)S(1)} %collective-permute-done.13), channel_id=1, source_target_pairs={{0,8},{8,16},{16,24},{24,28},{28,20},{20,12},{12,4},{4,0},{2,6},{1... | collective-permute-start | bytes 1572872 | tf_op jit(solution)/shard_map/ppermute | solution.py:366
  48.1 1.7 %collective-permute-start.16 = (bf16[2,512,256]{2,1,0:T(8,128)(2,1)S(1)}, bf16[2,512,256]{2,1,0:T(8,128)(2,1)S(1)}, u32[]{:S(2)}, u32[]{:S(2)}) collective-permute-start(bf16[2,512,256]{2,1,0:T(8,128)(2,1)S(1)} %collective-permute-done.13), channel_id=1, source_target_pairs={{0,2},{2,0},{8,10},{10,8},{16,18},{18,16},{24,26},{26,24},{28,30},... | collective-permute-start | bytes 1572872 | tf_op jit(solution)/shard_map/ppermute | solution.py:368
  49.8 2.5 %collective-permute-done.3 = bf16[2,512,256]{2,1,0:T(8,128)(2,1)S(1)} collective-permute-done((bf16[2,512,256]{2,1,0:T(8,128)(2,1)S(1)}, bf16[2,512,256]{2,1,0:T(8,128)(2,1)S(1)}, u32[]{:S(2)}, u32[]{:S(2)}) %collective-permute-start.3) | collective-permute-done | bytes 524320 | tf_op jit(solution)/shard_map/ppermute | solution.py:366
  52.3 1.0 collective-permute-start.6
  53.3 0.0 collective-permute-done.4
  53.3 1.1 %maximum_dynamic-update-slice_fusion = bf16[16,512,256]{2,1,0:T(8,128)(2,1)} fusion(bf16[16,512,256]{2,1,0:T(8,128)(2,1)} %get-tuple-element.21, bf16[2,512,256]{2,1,0:T(8,128)(2,1)S(1)} %collective-permute-done.4, bf16[2,512,256]{2,1,0:T(8,128)(2,1)S(1)} %collective-permute-done.2), kind=kLoop, calls=%fused_computation.1 | loop fusion | flops 2097152 | bytes 2097152 | tf_op jit(solution)/shard_map/dynamic_update_slice | solution.py:360
  54.4 1.7 %collective-permute-start.5 = (bf16[2,512,256]{2,1,0:T(8,128)(2,1)S(1)}, bf16[2,512,256]{2,1,0:T(8,128)(2,1)S(1)}, u32[]{:S(2)}, u32[]{:S(2)}) collective-permute-start(bf16[2,512,256]{2,1,0:T(8,128)(2,1)S(1)} %collective-permute-done.3), channel_id=1, source_target_pairs={{0,8},{8,16},{16,24},{24,28},{28,20},{20,12},{12,4},{4,0},{2,6},{1... | collective-permute-start | bytes 1572872 | tf_op jit(solution)/shard_map/ppermute | solution.py:366
  56.2 1.8 %collective-permute-done.15 = bf16[2,512,256]{2,1,0:T(8,128)(2,1)S(1)} collective-permute-done((bf16[2,512,256]{2,1,0:T(8,128)(2,1)S(1)}, bf16[2,512,256]{2,1,0:T(8,128)(2,1)S(1)}, u32[]{:S(2)}, u32[]{:S(2)}) %collective-permute-start.15) | collective-permute-done | bytes 524320 | tf_op jit(solution)/shard_map/ppermute | solution.py:366
  58.0 1.0 collective-permute-start.17
  58.9 0.0 collective-permute-done.16
  58.9 1.1 %maximum_dynamic-update-slice_fusion.4 = bf16[16,512,256]{2,1,0:T(8,128)(2,1)} fusion(bf16[16,512,256]{2,1,0:T(8,128)(2,1)} %maximum_dynamic-update-slice_fusion.3, bf16[2,512,256]{2,1,0:T(8,128)(2,1)S(1)} %collective-permute-done.16, bf16[2,512,256]{2,1,0:T(8,128)(2,1)S(1)} %collective-permute-done.13), kind=kLoop, calls=%fused_computation.5 | loop fusion | flops 2097152 | bytes 2097152 | tf_op jit(solution)/shard_map/dynamic_update_slice | solution.py:360
  60.0 1.8 %collective-permute-start.18 = (bf16[1,512,256]{2,1,0:T(8,128)(2,1)S(1)}, bf16[1,512,256]{2,1,0:T(8,128)(2,1)S(1)}, u32[]{:S(2)}, u32[]{:S(2)}) collective-permute-start(bf16[1,512,256]{2,1,0:T(8,128)(2,1)S(1)} %slice.7), channel_id=1, source_target_pairs={{0,8},{8,16},{16,24},{24,28},{28,20},{20,12},{12,4},{4,0},{2,6},{1... | collective-permute-start | bytes 786440 | tf_op jit(solution)/shard_map/ppermute | solution.py:366
  61.8 0.0 collective-permute-done.6
  61.8 1.0 %maximum_dynamic-update-slice_fusion.1 = bf16[16,512,256]{2,1,0:T(8,128)(2,1)} fusion(bf16[16,512,256]{2,1,0:T(8,128)(2,1)} %maximum_dynamic-update-slice_fusion, bf16[2,512,256]{2,1,0:T(8,128)(2,1)S(1)} %collective-permute-done.6, bf16[2,512,256]{2,1,0:T(8,128)(2,1)S(1)} %collective-permute-done.3), kind=kLoop, calls=%fused_computation.2 | loop fusion | flops 2097152 | bytes 2097152 | tf_op jit(solution)/shard_map/dynamic_update_slice | solution.py:360
  62.9 0.7 collective-permute-done.5
  63.6 1.4 %collective-permute-start.8 = (bf16[1,512,256]{2,1,0:T(8,128)(2,1)S(1)}, bf16[1,512,256]{2,1,0:T(8,128)(2,1)S(1)}, u32[]{:S(2)}, u32[]{:S(2)}) collective-permute-start(bf16[1,512,256]{2,1,0:T(8,128)(2,1)S(1)} %slice.6), channel_id=1, source_target_pairs={{0,8},{8,16},{16,24},{24,28},{28,20},{20,12},{12,4},{4,0},{2,6},{1... | collective-permute-start | bytes 786440 | tf_op jit(solution)/shard_map/ppermute | solution.py:366
  65.0 1.7 %collective-permute-start.7 = (bf16[2,512,256]{2,1,0:T(8,128)(2,1)S(1)}, bf16[2,512,256]{2,1,0:T(8,128)(2,1)S(1)}, u32[]{:S(2)}, u32[]{:S(2)}) collective-permute-start(bf16[2,512,256]{2,1,0:T(8,128)(2,1)S(1)} %collective-permute-done.5), channel_id=1, source_target_pairs={{0,2},{2,0},{8,10},{10,8},{16,18},{18,16},{24,26},{26,24},{28,30},... | collective-permute-start | bytes 1572872 | tf_op jit(solution)/shard_map/ppermute | solution.py:368
  66.7 0.0 collective-permute-done.18
  66.7 0.6 collective-permute-start.19
  67.4 0.7 copy.9.pairs_ref
  68.0 1.3 %fusion.slot_ref = s32[16]{0:T(128)} fusion(s32[16,16]{1,0:T(8,128)} %constant.34.clone, s32[]{:T(128)S(6)} %select_n.3), kind=kLoop, calls=%fused_computation.15 | loop fusion | bytes 132 | tf_op jit(solution)/shard_map/squeeze | solution.py:448
  69.3 0.0 collective-permute-done.8
  69.3 1.7 %collective-permute-start.9 = (bf16[1,512,256]{2,1,0:T(8,128)(2,1)S(1)}, bf16[1,512,256]{2,1,0:T(8,128)(2,1)S(1)}, u32[]{:S(2)}, u32[]{:S(2)}) collective-permute-start(bf16[1,512,256]{2,1,0:T(8,128)(2,1)S(1)} %collective-permute-done.8), channel_id=1, source_target_pairs={{0,2},{2,0},{8,10},{10,8},{16,18},{18,16},{24,26},{26,24},{28,30},... | collective-permute-start | bytes 786440 | tf_op jit(solution)/shard_map/ppermute | solution.py:368
  71.0 0.0 collective-permute-done.17
  71.0 1.0 %maximum_dynamic-update-slice_fusion.5 = bf16[16,512,256]{2,1,0:T(8,128)(2,1)} fusion(bf16[16,512,256]{2,1,0:T(8,128)(2,1)} %maximum_dynamic-update-slice_fusion.4, bf16[2,512,256]{2,1,0:T(8,128)(2,1)S(1)} %collective-permute-done.17, bf16[2,512,256]{2,1,0:T(8,128)(2,1)S(1)} %collective-permute-done.15), kind=kLoop, calls=%fused_computation.6 | loop fusion | flops 2097152 | bytes 2097152 | tf_op jit(solution)/shard_map/dynamic_update_slice | solution.py:360
  72.0 0.0 collective-permute-done.19
  72.0 0.9 maximum_dynamic-update-slice_fusion.7.refs_1_
  72.9 0.0 collective-permute-done.7
  72.9 1.0 %maximum_dynamic-update-slice_fusion.2 = bf16[16,512,256]{2,1,0:T(8,128)(2,1)} fusion(bf16[16,512,256]{2,1,0:T(8,128)(2,1)} %maximum_dynamic-update-slice_fusion.1, bf16[2,512,256]{2,1,0:T(8,128)(2,1)S(1)} %collective-permute-done.7, bf16[2,512,256]{2,1,0:T(8,128)(2,1)S(1)} %collective-permute-done.5), kind=kLoop, calls=%fused_computation.3 | loop fusion | flops 2097152 | bytes 2097152 | tf_op jit(solution)/shard_map/dynamic_update_slice | solution.py:360
  74.0 0.0 collective-permute-done.9
  74.0 0.8 maximum_dynamic-update-slice_fusion.6.refs_0_
  74.8 24.9 %cross_spectra.1 = bf16[8,32,32,16,128]{4,3,2,1,0:T(8,128)(2,1)} custom-call(s32[8,2]{1,0:T(8,128)} %copy.9.pairs_ref, s32[16]{0:T(128)} %fusion.slot_ref, bf16[16,512,256]{2,1,0:T(8,128)(2,1)} %maximum_dynamic-update-slice_fusion.6.refs_0_, bf16[16,512,256]{2,1,0:T(8,128)(2,1)} %maximum_dynamic-update-slice_fusion.7.refs_1_), custom_call_target="tpu_custom_call" | custom-call | tf_op jit(solution)/shard_map/cross_spectra/pallas_call | solution.py:317
  (11 shorter events, 0.0 us)
Async XLA Ops:
  0.0 1.6 %copy-start = (bf16[64,4,4096]{2,1,0:T(4,128)(2,1)S(1)}, bf16[64,4,4096]{2,1,0:T(4,128)(2,1)}, u32[]{:S(2)}) copy-start(bf16[64,4,4096]{2,1,0:T(4,128)(2,1)} %param.8) | copy-start | bytes 6291460
  0.0 3.3 %copy-start.3 = (bf16[384,256]{1,0:T(8,128)(2,1)S(1)}, bf16[384,256]{1,0:T(8,128)(2,1)}, u32[]{:S(2)}) copy-start(bf16[384,256]{1,0:T(8,128)(2,1)} %constant.32.clone.inner_ref) | copy-start | bytes 589828
  0.0 3.4 %copy-start.4 = (bf16[128,128]{1,0:T(8,128)(2,1)S(1)}, bf16[128,128]{1,0:T(8,128)(2,1)}, u32[]{:S(2)}) copy-start(bf16[128,128]{1,0:T(8,128)(2,1)} %constant.31.clone.order_ref) | copy-start | bytes 98308
  0.0 13.8 %copy-start.2 = (bf16[128,256]{1,0:T(8,128)(2,1)S(1)}, bf16[128,256]{1,0:T(8,128)(2,1)}, u32[]{:S(2)}) copy-start(bf16[128,256]{1,0:T(8,128)(2,1)} %constant.33.clone.first_ref) | copy-start | bytes 196612
  5.3 8.5 %collective-permute-start.10 = (bf16[64,2176]{1,0:T(8,128)(2,1)S(1)}, bf16[64,2176]{1,0:T(8,128)(2,1)S(1)}, u32[]{:S(2)}, u32[]{:S(2)}) collective-permute-start(bf16[64,2176]{1,0:T(8,128)(2,1)S(1)} %get-tuple-element.26.own_ref), channel_id=1, source_target_pairs={{0,1},{1,0},{2,3},{3,2},{4,5},{5,4},{6,7},{7,6},{8,9},{9,8},{10,11... | collective-permute-start | bytes 835592 | tf_op jit(solution)/shard_map/ppermute | solution.py:421
  7.4 13.4 %collective-permute-start = (bf16[64,2176]{1,0:T(8,128)(2,1)S(1)}, bf16[64,2176]{1,0:T(8,128)(2,1)S(1)}, u32[]{:S(2)}, u32[]{:S(2)}) collective-permute-start(bf16[64,2176]{1,0:T(8,128)(2,1)S(1)} %get-tuple-element.19.own_ref), channel_id=1, source_target_pairs={{0,1},{1,0},{2,3},{3,2},{4,5},{5,4},{6,7},{7,6},{8,9},{9,8},{10,11... | collective-permute-start | bytes 835592 | tf_op jit(solution)/shard_map/ppermute | solution.py:421
  18.7 7.3 %collective-permute-start.11 = (bf16[1,512,256]{2,1,0:T(8,128)(2,1)S(1)}, bf16[1,512,256]{2,1,0:T(8,128)(2,1)S(1)}, u32[]{:S(2)}, u32[]{:S(2)}) collective-permute-start(bf16[1,512,256]{2,1,0:T(8,128)(2,1)S(1)} %whiten.3), channel_id=1, source_target_pairs={{0,2},{2,0},{8,10},{10,8},{16,18},{18,16},{24,26},{26,24},{28,30},... | collective-permute-start | bytes 786440 | tf_op jit(solution)/shard_map/ppermute | solution.py:355
  25.8 2.8 %collective-permute-start.1 = (bf16[1,512,256]{2,1,0:T(8,128)(2,1)S(1)}, bf16[1,512,256]{2,1,0:T(8,128)(2,1)S(1)}, u32[]{:S(2)}, u32[]{:S(2)}) collective-permute-start(bf16[1,512,256]{2,1,0:T(8,128)(2,1)S(1)} %whiten.2), channel_id=1, source_target_pairs={{0,2},{2,0},{8,10},{10,8},{16,18},{18,16},{24,26},{26,24},{28,30},... | collective-permute-start | bytes 786440 | tf_op jit(solution)/shard_map/ppermute | solution.py:355
  26.9 8.6 %collective-permute-start.12 = (bf16[2,512,256]{2,1,0:T(8,128)(2,1)S(1)}, bf16[2,512,256]{2,1,0:T(8,128)(2,1)S(1)}, u32[]{:S(2)}, u32[]{:S(2)}) collective-permute-start(bf16[2,512,256]{2,1,0:T(8,128)(2,1)S(1)} %get-tuple-element.34), channel_id=1, source_target_pairs={{0,8},{8,16},{16,24},{24,28},{28,20},{20,12},{12,4},{4,0},{2,6},{1... | collective-permute-start | bytes 1572872 | tf_op jit(solution)/shard_map/ppermute | solution.py:366
  29.4 11.7 %collective-permute-start.2 = (bf16[2,512,256]{2,1,0:T(8,128)(2,1)S(1)}, bf16[2,512,256]{2,1,0:T(8,128)(2,1)S(1)}, u32[]{:S(2)}, u32[]{:S(2)}) collective-permute-start(bf16[2,512,256]{2,1,0:T(8,128)(2,1)S(1)} %get-tuple-element.36), channel_id=1, source_target_pairs={{0,8},{8,16},{16,24},{24,28},{28,20},{20,12},{12,4},{4,0},{2,6},{1... | collective-permute-start | bytes 1572872 | tf_op jit(solution)/shard_map/ppermute | solution.py:366
  35.5 8.7 %collective-permute-start.14 = (bf16[2,512,256]{2,1,0:T(8,128)(2,1)S(1)}, bf16[2,512,256]{2,1,0:T(8,128)(2,1)S(1)}, u32[]{:S(2)}, u32[]{:S(2)}) collective-permute-start(bf16[2,512,256]{2,1,0:T(8,128)(2,1)S(1)} %collective-permute-done.12), channel_id=1, source_target_pairs={{0,2},{2,0},{8,10},{10,8},{16,18},{18,16},{24,26},{26,24},{28,30},... | collective-permute-start | bytes 1572872 | tf_op jit(solution)/shard_map/ppermute | solution.py:368
  36.5 10.3 %collective-permute-start.13 = (bf16[2,512,256]{2,1,0:T(8,128)(2,1)S(1)}, bf16[2,512,256]{2,1,0:T(8,128)(2,1)S(1)}, u32[]{:S(2)}, u32[]{:S(2)}) collective-permute-start(bf16[2,512,256]{2,1,0:T(8,128)(2,1)S(1)} %collective-permute-done.12), channel_id=1, source_target_pairs={{0,8},{8,16},{16,24},{24,28},{28,20},{20,12},{12,4},{4,0},{2,6},{1... | collective-permute-start | bytes 1572872 | tf_op jit(solution)/shard_map/ppermute | solution.py:366
  41.1 11.2 %collective-permute-start.3 = (bf16[2,512,256]{2,1,0:T(8,128)(2,1)S(1)}, bf16[2,512,256]{2,1,0:T(8,128)(2,1)S(1)}, u32[]{:S(2)}, u32[]{:S(2)}) collective-permute-start(bf16[2,512,256]{2,1,0:T(8,128)(2,1)S(1)} %collective-permute-done.2), channel_id=1, source_target_pairs={{0,8},{8,16},{16,24},{24,28},{28,20},{20,12},{12,4},{4,0},{2,6},{1... | collective-permute-start | bytes 1572872 | tf_op jit(solution)/shard_map/ppermute | solution.py:366
  42.5 10.8 %collective-permute-start.4 = (bf16[2,512,256]{2,1,0:T(8,128)(2,1)S(1)}, bf16[2,512,256]{2,1,0:T(8,128)(2,1)S(1)}, u32[]{:S(2)}, u32[]{:S(2)}) collective-permute-start(bf16[2,512,256]{2,1,0:T(8,128)(2,1)S(1)} %collective-permute-done.2), channel_id=1, source_target_pairs={{0,2},{2,0},{8,10},{10,8},{16,18},{18,16},{24,26},{26,24},{28,30},... | collective-permute-start | bytes 1572872 | tf_op jit(solution)/shard_map/ppermute | solution.py:368
  45.3 22.1 %copy-start.5 = (s32[8,2]{0,1:T(2,128)S(1)}, s32[8,2]{0,1:T(2,128)}, u32[]{:S(2)}) copy-start(s32[8,2]{0,1:T(2,128)} %param.10) | copy-start | bytes 196
  46.7 11.2 %collective-permute-start.15 = (bf16[2,512,256]{2,1,0:T(8,128)(2,1)S(1)}, bf16[2,512,256]{2,1,0:T(8,128)(2,1)S(1)}, u32[]{:S(2)}, u32[]{:S(2)}) collective-permute-start(bf16[2,512,256]{2,1,0:T(8,128)(2,1)S(1)} %collective-permute-done.13), channel_id=1, source_target_pairs={{0,8},{8,16},{16,24},{24,28},{28,20},{20,12},{12,4},{4,0},{2,6},{1... | collective-permute-start | bytes 1572872 | tf_op jit(solution)/shard_map/ppermute | solution.py:366
  48.1 10.8 %collective-permute-start.16 = (bf16[2,512,256]{2,1,0:T(8,128)(2,1)S(1)}, bf16[2,512,256]{2,1,0:T(8,128)(2,1)S(1)}, u32[]{:S(2)}, u32[]{:S(2)}) collective-permute-start(bf16[2,512,256]{2,1,0:T(8,128)(2,1)S(1)} %collective-permute-done.13), channel_id=1, source_target_pairs={{0,2},{2,0},{8,10},{10,8},{16,18},{18,16},{24,26},{26,24},{28,30},... | collective-permute-start | bytes 1572872 | tf_op jit(solution)/shard_map/ppermute | solution.py:368
  52.3 9.5 %collective-permute-start.6 = (bf16[2,512,256]{2,1,0:T(8,128)(2,1)S(1)}, bf16[2,512,256]{2,1,0:T(8,128)(2,1)S(1)}, u32[]{:S(2)}, u32[]{:S(2)}) collective-permute-start(bf16[2,512,256]{2,1,0:T(8,128)(2,1)S(1)} %collective-permute-done.3), channel_id=1, source_target_pairs={{0,2},{2,0},{8,10},{10,8},{16,18},{18,16},{24,26},{26,24},{28,30},... | collective-permute-start | bytes 1572872 | tf_op jit(solution)/shard_map/ppermute | solution.py:368
  54.4 9.2 %collective-permute-start.5 = (bf16[2,512,256]{2,1,0:T(8,128)(2,1)S(1)}, bf16[2,512,256]{2,1,0:T(8,128)(2,1)S(1)}, u32[]{:S(2)}, u32[]{:S(2)}) collective-permute-start(bf16[2,512,256]{2,1,0:T(8,128)(2,1)S(1)} %collective-permute-done.3), channel_id=1, source_target_pairs={{0,8},{8,16},{16,24},{24,28},{28,20},{20,12},{12,4},{4,0},{2,6},{1... | collective-permute-start | bytes 1572872 | tf_op jit(solution)/shard_map/ppermute | solution.py:366
  58.0 13.0 %collective-permute-start.17 = (bf16[2,512,256]{2,1,0:T(8,128)(2,1)S(1)}, bf16[2,512,256]{2,1,0:T(8,128)(2,1)S(1)}, u32[]{:S(2)}, u32[]{:S(2)}) collective-permute-start(bf16[2,512,256]{2,1,0:T(8,128)(2,1)S(1)} %collective-permute-done.15), channel_id=1, source_target_pairs={{0,2},{2,0},{8,10},{10,8},{16,18},{18,16},{24,26},{26,24},{28,30},... | collective-permute-start | bytes 1572872 | tf_op jit(solution)/shard_map/ppermute | solution.py:368
  60.0 6.7 %collective-permute-start.18 = (bf16[1,512,256]{2,1,0:T(8,128)(2,1)S(1)}, bf16[1,512,256]{2,1,0:T(8,128)(2,1)S(1)}, u32[]{:S(2)}, u32[]{:S(2)}) collective-permute-start(bf16[1,512,256]{2,1,0:T(8,128)(2,1)S(1)} %slice.7), channel_id=1, source_target_pairs={{0,8},{8,16},{16,24},{24,28},{28,20},{20,12},{12,4},{4,0},{2,6},{1... | collective-permute-start | bytes 786440 | tf_op jit(solution)/shard_map/ppermute | solution.py:366
  63.6 5.7 %collective-permute-start.8 = (bf16[1,512,256]{2,1,0:T(8,128)(2,1)S(1)}, bf16[1,512,256]{2,1,0:T(8,128)(2,1)S(1)}, u32[]{:S(2)}, u32[]{:S(2)}) collective-permute-start(bf16[1,512,256]{2,1,0:T(8,128)(2,1)S(1)} %slice.6), channel_id=1, source_target_pairs={{0,8},{8,16},{16,24},{24,28},{28,20},{20,12},{12,4},{4,0},{2,6},{1... | collective-permute-start | bytes 786440 | tf_op jit(solution)/shard_map/ppermute | solution.py:366
  65.0 7.9 %collective-permute-start.7 = (bf16[2,512,256]{2,1,0:T(8,128)(2,1)S(1)}, bf16[2,512,256]{2,1,0:T(8,128)(2,1)S(1)}, u32[]{:S(2)}, u32[]{:S(2)}) collective-permute-start(bf16[2,512,256]{2,1,0:T(8,128)(2,1)S(1)} %collective-permute-done.5), channel_id=1, source_target_pairs={{0,2},{2,0},{8,10},{10,8},{16,18},{18,16},{24,26},{26,24},{28,30},... | collective-permute-start | bytes 1572872 | tf_op jit(solution)/shard_map/ppermute | solution.py:368
  66.7 5.3 %collective-permute-start.19 = (bf16[1,512,256]{2,1,0:T(8,128)(2,1)S(1)}, bf16[1,512,256]{2,1,0:T(8,128)(2,1)S(1)}, u32[]{:S(2)}, u32[]{:S(2)}) collective-permute-start(bf16[1,512,256]{2,1,0:T(8,128)(2,1)S(1)} %collective-permute-done.18), channel_id=1, source_target_pairs={{0,2},{2,0},{8,10},{10,8},{16,18},{18,16},{24,26},{26,24},{28,30},... | collective-permute-start | bytes 786440 | tf_op jit(solution)/shard_map/ppermute | solution.py:368
  69.3 4.7 %collective-permute-start.9 = (bf16[1,512,256]{2,1,0:T(8,128)(2,1)S(1)}, bf16[1,512,256]{2,1,0:T(8,128)(2,1)S(1)}, u32[]{:S(2)}, u32[]{:S(2)}) collective-permute-start(bf16[1,512,256]{2,1,0:T(8,128)(2,1)S(1)} %collective-permute-done.8), channel_id=1, source_target_pairs={{0,2},{2,0},{8,10},{10,8},{16,18},{18,16},{24,26},{26,24},{28,30},... | collective-permute-start | bytes 786440 | tf_op jit(solution)/shard_map/ppermute | solution.py:368
  74.8 24.9 %copy-start.1 = (bf16[64,4,4096]{2,1,0:T(4,128)(2,1)S(1)}, bf16[64,4,4096]{2,1,0:T(4,128)(2,1)}, u32[]{:S(2)}) copy-start(bf16[64,4,4096]{2,1,0:T(4,128)(2,1)} %param.8) | copy-start | bytes 6291460

commit v2 on v1

--- a/solution.py
+++ b/solution.py
@@ -19,8 +19,8 @@
 EPSILON = 1e-06
 LANES = 128
 CHUNKS = (16, 16)
-TILE = (4, 32)
-PIECE = 4
+TILE = (8, 32)
+PIECE = (2, 2)
 TURNS = 4
 WHITEN_BYTES = 40_000_000
 VMEM_CROSS = 56
@@ -251,18 +251,20 @@
         copy.wait()
     lax.fori_loop(0, channels, first_pair, 0)
 
+    piece_rows, piece_cols = PIECE
+
     def piece(s, turn, a0, a, b0):
-        total = [[None] * PIECE for _ in range(PIECE)]
+        total = [[None] * piece_cols for _ in range(piece_rows)]
         for w in range(WIN):
-            straight = [planes_ref[s, 0, a0 + a + k, w] for k in range(PIECE)]
-            turned = [planes_ref[s, 1, a0 + a + k, w] for k in range(PIECE)]
-            for m in range(PIECE):
+            straight = [planes_ref[s, 0, a0 + a + k, w] for k in range(piece_rows)]
+            turned = [planes_ref[s, 1, a0 + a + k, w] for k in range(piece_rows)]
+            for m in range(piece_cols):
                 real, imag = planes_ref[s, 2, b0 + m, w], planes_ref[s, 3, b0 + m, w]
-                for k in range(PIECE):
+                for k in range(piece_rows):
                     term = straight[k] * real + turned[k] * imag
                     total[k][m] = term if w == 0 else total[k][m] + term
-        for k in range(PIECE):
-            for m in range(PIECE):
+        for k in range(piece_rows):
+            for m in range(piece_cols):
                 result_ref[turn, a + k, b0 + m, 0:8] = total[k][m][:, :LANES]
                 result_ref[turn, a + k, b0 + m, 8:16] = total[k][m][:, LANES:]
 
@@ -291,8 +293,8 @@
                 b0 = step * col_step
                 for k in range(ahead):
                     prepare(1 - s, (group * col_steps + step) * ahead + k)
-                for a in range(0, row_step, PIECE):
-                    for b in range(0, col_step, PIECE):
+                for a in range(0, row_step, piece_rows):
+                    for b in range(0, col_step, piece_cols):
                         piece(s, turn, a0, a, b0 + b)
                 return 0
 

time: 99.9 us -> 99 us (level)
  no operation moved by 1% of the time
where the time goes in v2:
time: 99 us; the launch traced here: 98.8 us
  Pallas kernels  35.7 us (36%)
  starting transfers between devices  27.2 us (27%)
  waiting for transfers between devices  20.5 us (21%)
  other arithmetic  10.7 us (11%)
  local copies, waits for them, and re-layouts  4.51 us (5%)
    pallas_call x1, Pallas kernels, cross_spectra(): pl.pallas_call(cross_kernel, in_specs=[smem, smem] + [hbm] * len(gathered...  24 us
    ppermute x8, waiting for transfers between devices, gather_blocks(): move(current[k][:1] if step == steps else current[k], perm=ring)  14.2 us
    ppermute x8, starting transfers between devices, gather_blocks(): move(current[k][:1] if step == steps else current[k], perm=ring)  12.4 us
    ppermute x8, starting transfers between devices, gather_blocks(): waiting[k] = ([current[k], move(current[k], perm=swap)], 4 * step - 2)  10.3 us
    dynamic_update_slice x10, other arithmetic, put(): gathered[k] = lax.dynamic_update_slice(gathered[k], piece, (slot, 0, 0))  9.92 us
    pallas_call x2, Pallas kernels, whiten(): pl.pallas_call(whiten_kernel, in_specs=[pl.BlockSpec(memory_space=pltpu.S...  9.82 us
    ppermute x2, waiting for transfers between devices, body(): lax.ppermute(message, 'band', [(0, 1), (1, 0)])  6.31 us
    ppermute x2, starting transfers between devices, gather_blocks(): move(own, perm=swap)  2.34 us
  transfers between devices with their start and end apart: 20, of which 7 were waited for; matrix products, arithmetic and copies ran while one was open for 11% of the time, Pallas kernels for 10%

profile of v2, /device:TPU:1, one launch (start us, length us, event | category | flops | bytes accessed | tf_op | source)
XLA Modules:
  0.0 98.8 jit_solution(6076815079419349439)
XLA Ops:
  0.0 0.0 copy-start
  0.0 0.0 copy-start.2
  0.0 0.8 pad_clamp_fusion
  0.8 0.8 copy-done
  1.6 1.4 %gather_fusion = bf16[32,4,4096]{2,1,0:T(4,128)(2,1)S(1)} fusion(bf16[64,4,4096]{2,1,0:T(4,128)(2,1)S(1)} %copy-done, s32[1024]{0:T(1024)S(1)} %pad_clamp_fusion), kind=kCustom, calls=%fused_computation | custom fusion | bytes 2097280 | tf_op jit(solution)/shard_map/gather | solution.py:415
  3.1 0.3 reshape.13.raw_ref
  3.3 0.0 copy-done.3
  3.4 1.9 %decimate.1 = (bf16[64,2176]{1,0:T(8,128)(2,1)S(1)}, bf16[64,2176]{1,0:T(8,128)(2,1)S(1)}) custom-call(bf16[128,128]{1,0:T(8,128)(2,1)S(1)} %copy-done.4, bf16[128,4096]{1,0:T(8,128)(2,1)S(1)} %reshape.13.raw_ref, bf16[384,256]{1,0:T(8,128)(2,1)S(1)} %copy-done.3), custom_call_target="tpu_custom_call" | custom-call | tf_op jit(solution)/shard_map/decimate/pallas_call | solution.py:417
  5.3 2.1 %collective-permute-start.10 = (bf16[64,2176]{1,0:T(8,128)(2,1)S(1)}, bf16[64,2176]{1,0:T(8,128)(2,1)S(1)}, u32[]{:S(2)}, u32[]{:S(2)}) collective-permute-start(bf16[64,2176]{1,0:T(8,128)(2,1)S(1)} %get-tuple-element.26.own_ref), channel_id=1, source_target_pairs={{0,1},{1,0},{2,3},{3,2},{4,5},{5,4},{6,7},{7,6},{8,9},{9,8},{10,11... | collective-permute-start | bytes 835592 | tf_op jit(solution)/shard_map/ppermute | solution.py:423
  7.4 0.1 collective-permute-start
  7.5 6.3 %collective-permute-done.10.other_ref = bf16[64,2176]{1,0:T(8,128)(2,1)S(1)} collective-permute-done((bf16[64,2176]{1,0:T(8,128)(2,1)S(1)}, bf16[64,2176]{1,0:T(8,128)(2,1)S(1)}, u32[]{:S(2)}, u32[]{:S(2)}) %collective-permute-start.10) | collective-permute-done | bytes 278560 | tf_op jit(solution)/shard_map/ppermute | solution.py:423
  13.8 4.9 %whiten.3 = bf16[1,512,256]{2,1,0:T(8,128)(2,1)S(1)} custom-call(s32[1]{0:T(128)} %bitcast.1.band_ref, bf16[64,2176]{1,0:T(8,128)(2,1)S(1)} %get-tuple-element.26.own_ref, bf16[64,2176]{1,0:T(8,128)(2,1)S(1)} %collective-permute-done.10.other_ref, bf16[128,256]{1,0:T(8,128)(2,1)S(1)} %copy-done.2, bf16[2,9,2048,256]{3,2,1,0:T(8,128)(2,1)} %constant.30.clone.table_ref), custom_call_target="tpu_custom_call" | custom-call | bytes 40000000 | tf_op jit(solution)/shard_map/whiten/pallas_call | solution.py:427
  18.7 2.1 %collective-permute-start.11 = (bf16[1,512,256]{2,1,0:T(8,128)(2,1)S(1)}, bf16[1,512,256]{2,1,0:T(8,128)(2,1)S(1)}, u32[]{:S(2)}, u32[]{:S(2)}) collective-permute-start(bf16[1,512,256]{2,1,0:T(8,128)(2,1)S(1)} %whiten.3), channel_id=1, source_target_pairs={{0,2},{2,0},{8,10},{10,8},{16,18},{18,16},{24,26},{26,24},{28,30},... | collective-permute-start | bytes 786440 | tf_op jit(solution)/shard_map/ppermute | solution.py:357
  20.8 0.0 collective-permute-done.other_ref
  20.9 4.9 %whiten.2 = bf16[1,512,256]{2,1,0:T(8,128)(2,1)S(1)} custom-call(s32[1]{0:T(128)} %bitcast.1.band_ref, bf16[64,2176]{1,0:T(8,128)(2,1)S(1)} %get-tuple-element.19.own_ref, bf16[64,2176]{1,0:T(8,128)(2,1)S(1)} %collective-permute-done.other_ref, bf16[128,256]{1,0:T(8,128)(2,1)S(1)} %copy-done.2, bf16[2,9,2048,256]{3,2,1,0:T(8,128)(2,1)} %constant.30.clone.table_ref), custom_call_target="tpu_custom_call" | custom-call | bytes 40000000 | tf_op jit(solution)/shard_map/whiten/pallas_call | solution.py:427
  25.8 0.2 collective-permute-start.1
  26.0 0.0 collective-permute-done.11
  26.0 0.9 constant_dynamic-update-slice_fusion
  26.9 1.6 %collective-permute-start.12 = (bf16[2,512,256]{2,1,0:T(8,128)(2,1)S(1)}, bf16[2,512,256]{2,1,0:T(8,128)(2,1)S(1)}, u32[]{:S(2)}, u32[]{:S(2)}) collective-permute-start(bf16[2,512,256]{2,1,0:T(8,128)(2,1)S(1)} %get-tuple-element.34), channel_id=1, source_target_pairs={{0,8},{8,16},{16,24},{24,28},{28,20},{20,12},{12,4},{4,0},{2,6},{1... | collective-permute-start | bytes 1572872 | tf_op jit(solution)/shard_map/ppermute | solution.py:368
  28.5 0.0 collective-permute-done.1
  28.5 0.9 constant_dynamic-update-slice_fusion.1
  29.4 1.3 %collective-permute-start.2 = (bf16[2,512,256]{2,1,0:T(8,128)(2,1)S(1)}, bf16[2,512,256]{2,1,0:T(8,128)(2,1)S(1)}, u32[]{:S(2)}, u32[]{:S(2)}) collective-permute-start(bf16[2,512,256]{2,1,0:T(8,128)(2,1)S(1)} %get-tuple-element.36), channel_id=1, source_target_pairs={{0,8},{8,16},{16,24},{24,28},{28,20},{20,12},{12,4},{4,0},{2,6},{1... | collective-permute-start | bytes 1572872 | tf_op jit(solution)/shard_map/ppermute | solution.py:368
  30.7 4.8 %collective-permute-done.12 = bf16[2,512,256]{2,1,0:T(8,128)(2,1)S(1)} collective-permute-done((bf16[2,512,256]{2,1,0:T(8,128)(2,1)S(1)}, bf16[2,512,256]{2,1,0:T(8,128)(2,1)S(1)}, u32[]{:S(2)}, u32[]{:S(2)}) %collective-permute-start.12) | collective-permute-done | bytes 524320 | tf_op jit(solution)/shard_map/ppermute | solution.py:368
  35.5 1.0 collective-permute-start.14
  36.5 1.7 %collective-permute-start.13 = (bf16[2,512,256]{2,1,0:T(8,128)(2,1)S(1)}, bf16[2,512,256]{2,1,0:T(8,128)(2,1)S(1)}, u32[]{:S(2)}, u32[]{:S(2)}) collective-permute-start(bf16[2,512,256]{2,1,0:T(8,128)(2,1)S(1)} %collective-permute-done.12), channel_id=1, source_target_pairs={{0,8},{8,16},{16,24},{24,28},{28,20},{20,12},{12,4},{4,0},{2,6},{1... | collective-permute-start | bytes 1572872 | tf_op jit(solution)/shard_map/ppermute | solution.py:368
  38.2 2.9 %collective-permute-done.2 = bf16[2,512,256]{2,1,0:T(8,128)(2,1)S(1)} collective-permute-done((bf16[2,512,256]{2,1,0:T(8,128)(2,1)S(1)}, bf16[2,512,256]{2,1,0:T(8,128)(2,1)S(1)}, u32[]{:S(2)}, u32[]{:S(2)}) %collective-permute-start.2) | collective-permute-done | bytes 524320 | tf_op jit(solution)/shard_map/ppermute | solution.py:368
  41.1 1.4 %collective-permute-start.3 = (bf16[2,512,256]{2,1,0:T(8,128)(2,1)S(1)}, bf16[2,512,256]{2,1,0:T(8,128)(2,1)S(1)}, u32[]{:S(2)}, u32[]{:S(2)}) collective-permute-start(bf16[2,512,256]{2,1,0:T(8,128)(2,1)S(1)} %collective-permute-done.2), channel_id=1, source_target_pairs={{0,8},{8,16},{16,24},{24,28},{28,20},{20,12},{12,4},{4,0},{2,6},{1... | collective-permute-start | bytes 1572872 | tf_op jit(solution)/shard_map/ppermute | solution.py:368
  42.5 1.7 %collective-permute-start.4 = (bf16[2,512,256]{2,1,0:T(8,128)(2,1)S(1)}, bf16[2,512,256]{2,1,0:T(8,128)(2,1)S(1)}, u32[]{:S(2)}, u32[]{:S(2)}) collective-permute-start(bf16[2,512,256]{2,1,0:T(8,128)(2,1)S(1)} %collective-permute-done.2), channel_id=1, source_target_pairs={{0,2},{2,0},{8,10},{10,8},{16,18},{18,16},{24,26},{26,24},{28,30},... | collective-permute-start | bytes 1572872 | tf_op jit(solution)/shard_map/ppermute | solution.py:370
  44.2 0.0 collective-permute-done.14
  44.2 1.1 %maximum_dynamic-update-slice_fusion.3 = bf16[16,512,256]{2,1,0:T(8,128)(2,1)} fusion(bf16[16,512,256]{2,1,0:T(8,128)(2,1)} %get-tuple-element.28, bf16[2,512,256]{2,1,0:T(8,128)(2,1)S(1)} %collective-permute-done.14, bf16[2,512,256]{2,1,0:T(8,128)(2,1)S(1)} %collective-permute-done.12), kind=kLoop, calls=%fused_computation.4 | loop fusion | flops 2097152 | bytes 2097152 | tf_op jit(solution)/shard_map/dynamic_update_slice | solution.py:362
  45.3 1.5 %collective-permute-done.13 = bf16[2,512,256]{2,1,0:T(8,128)(2,1)S(1)} collective-permute-done((bf16[2,512,256]{2,1,0:T(8,128)(2,1)S(1)}, bf16[2,512,256]{2,1,0:T(8,128)(2,1)S(1)}, u32[]{:S(2)}, u32[]{:S(2)}) %collective-permute-start.13) | collective-permute-done | bytes 524320 | tf_op jit(solution)/shard_map/ppermute | solution.py:368
  46.7 1.4 %collective-permute-start.15 = (bf16[2,512,256]{2,1,0:T(8,128)(2,1)S(1)}, bf16[2,512,256]{2,1,0:T(8,128)(2,1)S(1)}, u32[]{:S(2)}, u32[]{:S(2)}) collective-permute-start(bf16[2,512,256]{2,1,0:T(8,128)(2,1)S(1)} %collective-permute-done.13), channel_id=1, source_target_pairs={{0,8},{8,16},{16,24},{24,28},{28,20},{20,12},{12,4},{4,0},{2,6},{1... | collective-permute-start | bytes 1572872 | tf_op jit(solution)/shard_map/ppermute | solution.py:368
  48.1 1.7 %collective-permute-start.16 = (bf16[2,512,256]{2,1,0:T(8,128)(2,1)S(1)}, bf16[2,512,256]{2,1,0:T(8,128)(2,1)S(1)}, u32[]{:S(2)}, u32[]{:S(2)}) collective-permute-start(bf16[2,512,256]{2,1,0:T(8,128)(2,1)S(1)} %collective-permute-done.13), channel_id=1, source_target_pairs={{0,2},{2,0},{8,10},{10,8},{16,18},{18,16},{24,26},{26,24},{28,30},... | collective-permute-start | bytes 1572872 | tf_op jit(solution)/shard_map/ppermute | solution.py:370
  49.8 2.5 %collective-permute-done.3 = bf16[2,512,256]{2,1,0:T(8,128)(2,1)S(1)} collective-permute-done((bf16[2,512,256]{2,1,0:T(8,128)(2,1)S(1)}, bf16[2,512,256]{2,1,0:T(8,128)(2,1)S(1)}, u32[]{:S(2)}, u32[]{:S(2)}) %collective-permute-start.3) | collective-permute-done | bytes 524320 | tf_op jit(solution)/shard_map/ppermute | solution.py:368
  52.3 1.0 collective-permute-start.6
  53.3 0.0 collective-permute-done.4
  53.3 1.1 %maximum_dynamic-update-slice_fusion = bf16[16,512,256]{2,1,0:T(8,128)(2,1)} fusion(bf16[16,512,256]{2,1,0:T(8,128)(2,1)} %get-tuple-element.21, bf16[2,512,256]{2,1,0:T(8,128)(2,1)S(1)} %collective-permute-done.4, bf16[2,512,256]{2,1,0:T(8,128)(2,1)S(1)} %collective-permute-done.2), kind=kLoop, calls=%fused_computation.1 | loop fusion | flops 2097152 | bytes 2097152 | tf_op jit(solution)/shard_map/dynamic_update_slice | solution.py:362
  54.4 1.7 %collective-permute-start.5 = (bf16[2,512,256]{2,1,0:T(8,128)(2,1)S(1)}, bf16[2,512,256]{2,1,0:T(8,128)(2,1)S(1)}, u32[]{:S(2)}, u32[]{:S(2)}) collective-permute-start(bf16[2,512,256]{2,1,0:T(8,128)(2,1)S(1)} %collective-permute-done.3), channel_id=1, source_target_pairs={{0,8},{8,16},{16,24},{24,28},{28,20},{20,12},{12,4},{4,0},{2,6},{1... | collective-permute-start | bytes 1572872 | tf_op jit(solution)/shard_map/ppermute | solution.py:368
  56.2 1.8 %collective-permute-done.15 = bf16[2,512,256]{2,1,0:T(8,128)(2,1)S(1)} collective-permute-done((bf16[2,512,256]{2,1,0:T(8,128)(2,1)S(1)}, bf16[2,512,256]{2,1,0:T(8,128)(2,1)S(1)}, u32[]{:S(2)}, u32[]{:S(2)}) %collective-permute-start.15) | collective-permute-done | bytes 524320 | tf_op jit(solution)/shard_map/ppermute | solution.py:368
  58.0 1.0 collective-permute-start.17
  58.9 0.0 collective-permute-done.16
  58.9 1.1 %maximum_dynamic-update-slice_fusion.4 = bf16[16,512,256]{2,1,0:T(8,128)(2,1)} fusion(bf16[16,512,256]{2,1,0:T(8,128)(2,1)} %maximum_dynamic-update-slice_fusion.3, bf16[2,512,256]{2,1,0:T(8,128)(2,1)S(1)} %collective-permute-done.16, bf16[2,512,256]{2,1,0:T(8,128)(2,1)S(1)} %collective-permute-done.13), kind=kLoop, calls=%fused_computation.5 | loop fusion | flops 2097152 | bytes 2097152 | tf_op jit(solution)/shard_map/dynamic_update_slice | solution.py:362
  60.0 1.8 %collective-permute-start.18 = (bf16[1,512,256]{2,1,0:T(8,128)(2,1)S(1)}, bf16[1,512,256]{2,1,0:T(8,128)(2,1)S(1)}, u32[]{:S(2)}, u32[]{:S(2)}) collective-permute-start(bf16[1,512,256]{2,1,0:T(8,128)(2,1)S(1)} %slice.7), channel_id=1, source_target_pairs={{0,8},{8,16},{16,24},{24,28},{28,20},{20,12},{12,4},{4,0},{2,6},{1... | collective-permute-start | bytes 786440 | tf_op jit(solution)/shard_map/ppermute | solution.py:368
  61.8 0.0 collective-permute-done.6
  61.8 1.0 %maximum_dynamic-update-slice_fusion.1 = bf16[16,512,256]{2,1,0:T(8,128)(2,1)} fusion(bf16[16,512,256]{2,1,0:T(8,128)(2,1)} %maximum_dynamic-update-slice_fusion, bf16[2,512,256]{2,1,0:T(8,128)(2,1)S(1)} %collective-permute-done.6, bf16[2,512,256]{2,1,0:T(8,128)(2,1)S(1)} %collective-permute-done.3), kind=kLoop, calls=%fused_computation.2 | loop fusion | flops 2097152 | bytes 2097152 | tf_op jit(solution)/shard_map/dynamic_update_slice | solution.py:362
  62.9 0.7 collective-permute-done.5
  63.6 1.4 %collective-permute-start.8 = (bf16[1,512,256]{2,1,0:T(8,128)(2,1)S(1)}, bf16[1,512,256]{2,1,0:T(8,128)(2,1)S(1)}, u32[]{:S(2)}, u32[]{:S(2)}) collective-permute-start(bf16[1,512,256]{2,1,0:T(8,128)(2,1)S(1)} %slice.6), channel_id=1, source_target_pairs={{0,8},{8,16},{16,24},{24,28},{28,20},{20,12},{12,4},{4,0},{2,6},{1... | collective-permute-start | bytes 786440 | tf_op jit(solution)/shard_map/ppermute | solution.py:368
  65.0 1.7 %collective-permute-start.7 = (bf16[2,512,256]{2,1,0:T(8,128)(2,1)S(1)}, bf16[2,512,256]{2,1,0:T(8,128)(2,1)S(1)}, u32[]{:S(2)}, u32[]{:S(2)}) collective-permute-start(bf16[2,512,256]{2,1,0:T(8,128)(2,1)S(1)} %collective-permute-done.5), channel_id=1, source_target_pairs={{0,2},{2,0},{8,10},{10,8},{16,18},{18,16},{24,26},{26,24},{28,30},... | collective-permute-start | bytes 1572872 | tf_op jit(solution)/shard_map/ppermute | solution.py:370
  66.7 0.0 collective-permute-done.18
  66.7 0.6 collective-permute-start.19
  67.4 0.7 copy.9.pairs_ref
  68.0 1.3 %fusion.slot_ref = s32[16]{0:T(128)} fusion(s32[16,16]{1,0:T(8,128)} %constant.34.clone, s32[]{:T(128)S(6)} %select_n.3), kind=kLoop, calls=%fused_computation.15 | loop fusion | bytes 132 | tf_op jit(solution)/shard_map/squeeze | solution.py:450
  69.3 0.0 collective-permute-done.8
  69.3 1.7 %collective-permute-start.9 = (bf16[1,512,256]{2,1,0:T(8,128)(2,1)S(1)}, bf16[1,512,256]{2,1,0:T(8,128)(2,1)S(1)}, u32[]{:S(2)}, u32[]{:S(2)}) collective-permute-start(bf16[1,512,256]{2,1,0:T(8,128)(2,1)S(1)} %collective-permute-done.8), channel_id=1, source_target_pairs={{0,2},{2,0},{8,10},{10,8},{16,18},{18,16},{24,26},{26,24},{28,30},... | collective-permute-start | bytes 786440 | tf_op jit(solution)/shard_map/ppermute | solution.py:370
  71.0 0.0 collective-permute-done.17
  71.0 1.0 %maximum_dynamic-update-slice_fusion.5 = bf16[16,512,256]{2,1,0:T(8,128)(2,1)} fusion(bf16[16,512,256]{2,1,0:T(8,128)(2,1)} %maximum_dynamic-update-slice_fusion.4, bf16[2,512,256]{2,1,0:T(8,128)(2,1)S(1)} %collective-permute-done.17, bf16[2,512,256]{2,1,0:T(8,128)(2,1)S(1)} %collective-permute-done.15), kind=kLoop, calls=%fused_computation.6 | loop fusion | flops 2097152 | bytes 2097152 | tf_op jit(solution)/shard_map/dynamic_update_slice | solution.py:362
  72.0 0.0 collective-permute-done.19
  72.0 0.9 maximum_dynamic-update-slice_fusion.7.refs_1_
  72.9 0.0 collective-permute-done.7
  72.9 1.0 %maximum_dynamic-update-slice_fusion.2 = bf16[16,512,256]{2,1,0:T(8,128)(2,1)} fusion(bf16[16,512,256]{2,1,0:T(8,128)(2,1)} %maximum_dynamic-update-slice_fusion.1, bf16[2,512,256]{2,1,0:T(8,128)(2,1)S(1)} %collective-permute-done.7, bf16[2,512,256]{2,1,0:T(8,128)(2,1)S(1)} %collective-permute-done.5), kind=kLoop, calls=%fused_computation.3 | loop fusion | flops 2097152 | bytes 2097152 | tf_op jit(solution)/shard_map/dynamic_update_slice | solution.py:362
  74.0 0.0 collective-permute-done.9
  74.0 0.8 maximum_dynamic-update-slice_fusion.6.refs_0_
  74.8 24.0 %cross_spectra.1 = bf16[8,32,32,16,128]{4,3,2,1,0:T(8,128)(2,1)} custom-call(s32[8,2]{1,0:T(8,128)} %copy.9.pairs_ref, s32[16]{0:T(128)} %fusion.slot_ref, bf16[16,512,256]{2,1,0:T(8,128)(2,1)} %maximum_dynamic-update-slice_fusion.6.refs_0_, bf16[16,512,256]{2,1,0:T(8,128)(2,1)} %maximum_dynamic-update-slice_fusion.7.refs_1_), custom_call_target="tpu_custom_call" | custom-call | tf_op jit(solution)/shard_map/cross_spectra/pallas_call | solution.py:319
  98.8 0.0 copy-done.1
  (11 shorter events, 0.0 us)
Async XLA Ops:
  0.0 1.6 %copy-start = (bf16[64,4,4096]{2,1,0:T(4,128)(2,1)S(1)}, bf16[64,4,4096]{2,1,0:T(4,128)(2,1)}, u32[]{:S(2)}) copy-start(bf16[64,4,4096]{2,1,0:T(4,128)(2,1)} %param.8) | copy-start | bytes 6291460
  0.0 3.3 %copy-start.3 = (bf16[384,256]{1,0:T(8,128)(2,1)S(1)}, bf16[384,256]{1,0:T(8,128)(2,1)}, u32[]{:S(2)}) copy-start(bf16[384,256]{1,0:T(8,128)(2,1)} %constant.32.clone.inner_ref) | copy-start | bytes 589828
  0.0 3.4 %copy-start.4 = (bf16[128,128]{1,0:T(8,128)(2,1)S(1)}, bf16[128,128]{1,0:T(8,128)(2,1)}, u32[]{:S(2)}) copy-start(bf16[128,128]{1,0:T(8,128)(2,1)} %constant.31.clone.order_ref) | copy-start | bytes 98308
  0.0 13.8 %copy-start.2 = (bf16[128,256]{1,0:T(8,128)(2,1)S(1)}, bf16[128,256]{1,0:T(8,128)(2,1)}, u32[]{:S(2)}) copy-start(bf16[128,256]{1,0:T(8,128)(2,1)} %constant.33.clone.first_ref) | copy-start | bytes 196612
  5.3 8.5 %collective-permute-start.10 = (bf16[64,2176]{1,0:T(8,128)(2,1)S(1)}, bf16[64,2176]{1,0:T(8,128)(2,1)S(1)}, u32[]{:S(2)}, u32[]{:S(2)}) collective-permute-start(bf16[64,2176]{1,0:T(8,128)(2,1)S(1)} %get-tuple-element.26.own_ref), channel_id=1, source_target_pairs={{0,1},{1,0},{2,3},{3,2},{4,5},{5,4},{6,7},{7,6},{8,9},{9,8},{10,11... | collective-permute-start | bytes 835592 | tf_op jit(solution)/shard_map/ppermute | solution.py:423
  7.4 13.4 %collective-permute-start = (bf16[64,2176]{1,0:T(8,128)(2,1)S(1)}, bf16[64,2176]{1,0:T(8,128)(2,1)S(1)}, u32[]{:S(2)}, u32[]{:S(2)}) collective-permute-start(bf16[64,2176]{1,0:T(8,128)(2,1)S(1)} %get-tuple-element.19.own_ref), channel_id=1, source_target_pairs={{0,1},{1,0},{2,3},{3,2},{4,5},{5,4},{6,7},{7,6},{8,9},{9,8},{10,11... | collective-permute-start | bytes 835592 | tf_op jit(solution)/shard_map/ppermute | solution.py:423
  18.7 7.3 %collective-permute-start.11 = (bf16[1,512,256]{2,1,0:T(8,128)(2,1)S(1)}, bf16[1,512,256]{2,1,0:T(8,128)(2,1)S(1)}, u32[]{:S(2)}, u32[]{:S(2)}) collective-permute-start(bf16[1,512,256]{2,1,0:T(8,128)(2,1)S(1)} %whiten.3), channel_id=1, source_target_pairs={{0,2},{2,0},{8,10},{10,8},{16,18},{18,16},{24,26},{26,24},{28,30},... | collective-permute-start | bytes 786440 | tf_op jit(solution)/shard_map/ppermute | solution.py:357
  25.8 2.8 %collective-permute-start.1 = (bf16[1,512,256]{2,1,0:T(8,128)(2,1)S(1)}, bf16[1,512,256]{2,1,0:T(8,128)(2,1)S(1)}, u32[]{:S(2)}, u32[]{:S(2)}) collective-permute-start(bf16[1,512,256]{2,1,0:T(8,128)(2,1)S(1)} %whiten.2), channel_id=1, source_target_pairs={{0,2},{2,0},{8,10},{10,8},{16,18},{18,16},{24,26},{26,24},{28,30},... | collective-permute-start | bytes 786440 | tf_op jit(solution)/shard_map/ppermute | solution.py:357
  26.9 8.6 %collective-permute-start.12 = (bf16[2,512,256]{2,1,0:T(8,128)(2,1)S(1)}, bf16[2,512,256]{2,1,0:T(8,128)(2,1)S(1)}, u32[]{:S(2)}, u32[]{:S(2)}) collective-permute-start(bf16[2,512,256]{2,1,0:T(8,128)(2,1)S(1)} %get-tuple-element.34), channel_id=1, source_target_pairs={{0,8},{8,16},{16,24},{24,28},{28,20},{20,12},{12,4},{4,0},{2,6},{1... | collective-permute-start | bytes 1572872 | tf_op jit(solution)/shard_map/ppermute | solution.py:368
  29.4 11.7 %collective-permute-start.2 = (bf16[2,512,256]{2,1,0:T(8,128)(2,1)S(1)}, bf16[2,512,256]{2,1,0:T(8,128)(2,1)S(1)}, u32[]{:S(2)}, u32[]{:S(2)}) collective-permute-start(bf16[2,512,256]{2,1,0:T(8,128)(2,1)S(1)} %get-tuple-element.36), channel_id=1, source_target_pairs={{0,8},{8,16},{16,24},{24,28},{28,20},{20,12},{12,4},{4,0},{2,6},{1... | collective-permute-start | bytes 1572872 | tf_op jit(solution)/shard_map/ppermute | solution.py:368
  35.5 8.7 %collective-permute-start.14 = (bf16[2,512,256]{2,1,0:T(8,128)(2,1)S(1)}, bf16[2,512,256]{2,1,0:T(8,128)(2,1)S(1)}, u32[]{:S(2)}, u32[]{:S(2)}) collective-permute-start(bf16[2,512,256]{2,1,0:T(8,128)(2,1)S(1)} %collective-permute-done.12), channel_id=1, source_target_pairs={{0,2},{2,0},{8,10},{10,8},{16,18},{18,16},{24,26},{26,24},{28,30},... | collective-permute-start | bytes 1572872 | tf_op jit(solution)/shard_map/ppermute | solution.py:370
  36.5 10.3 %collective-permute-start.13 = (bf16[2,512,256]{2,1,0:T(8,128)(2,1)S(1)}, bf16[2,512,256]{2,1,0:T(8,128)(2,1)S(1)}, u32[]{:S(2)}, u32[]{:S(2)}) collective-permute-start(bf16[2,512,256]{2,1,0:T(8,128)(2,1)S(1)} %collective-permute-done.12), channel_id=1, source_target_pairs={{0,8},{8,16},{16,24},{24,28},{28,20},{20,12},{12,4},{4,0},{2,6},{1... | collective-permute-start | bytes 1572872 | tf_op jit(solution)/shard_map/ppermute | solution.py:368
  41.1 11.2 %collective-permute-start.3 = (bf16[2,512,256]{2,1,0:T(8,128)(2,1)S(1)}, bf16[2,512,256]{2,1,0:T(8,128)(2,1)S(1)}, u32[]{:S(2)}, u32[]{:S(2)}) collective-permute-start(bf16[2,512,256]{2,1,0:T(8,128)(2,1)S(1)} %collective-permute-done.2), channel_id=1, source_target_pairs={{0,8},{8,16},{16,24},{24,28},{28,20},{20,12},{12,4},{4,0},{2,6},{1... | collective-permute-start | bytes 1572872 | tf_op jit(solution)/shard_map/ppermute | solution.py:368
  42.5 10.8 %collective-permute-start.4 = (bf16[2,512,256]{2,1,0:T(8,128)(2,1)S(1)}, bf16[2,512,256]{2,1,0:T(8,128)(2,1)S(1)}, u32[]{:S(2)}, u32[]{:S(2)}) collective-permute-start(bf16[2,512,256]{2,1,0:T(8,128)(2,1)S(1)} %collective-permute-done.2), channel_id=1, source_target_pairs={{0,2},{2,0},{8,10},{10,8},{16,18},{18,16},{24,26},{26,24},{28,30},... | collective-permute-start | bytes 1572872 | tf_op jit(solution)/shard_map/ppermute | solution.py:370
  45.3 22.1 %copy-start.5 = (s32[8,2]{0,1:T(2,128)S(1)}, s32[8,2]{0,1:T(2,128)}, u32[]{:S(2)}) copy-start(s32[8,2]{0,1:T(2,128)} %param.10) | copy-start | bytes 196
  46.7 11.2 %collective-permute-start.15 = (bf16[2,512,256]{2,1,0:T(8,128)(2,1)S(1)}, bf16[2,512,256]{2,1,0:T(8,128)(2,1)S(1)}, u32[]{:S(2)}, u32[]{:S(2)}) collective-permute-start(bf16[2,512,256]{2,1,0:T(8,128)(2,1)S(1)} %collective-permute-done.13), channel_id=1, source_target_pairs={{0,8},{8,16},{16,24},{24,28},{28,20},{20,12},{12,4},{4,0},{2,6},{1... | collective-permute-start | bytes 1572872 | tf_op jit(solution)/shard_map/ppermute | solution.py:368
  48.1 10.8 %collective-permute-start.16 = (bf16[2,512,256]{2,1,0:T(8,128)(2,1)S(1)}, bf16[2,512,256]{2,1,0:T(8,128)(2,1)S(1)}, u32[]{:S(2)}, u32[]{:S(2)}) collective-permute-start(bf16[2,512,256]{2,1,0:T(8,128)(2,1)S(1)} %collective-permute-done.13), channel_id=1, source_target_pairs={{0,2},{2,0},{8,10},{10,8},{16,18},{18,16},{24,26},{26,24},{28,30},... | collective-permute-start | bytes 1572872 | tf_op jit(solution)/shard_map/ppermute | solution.py:370
  52.3 9.5 %collective-permute-start.6 = (bf16[2,512,256]{2,1,0:T(8,128)(2,1)S(1)}, bf16[2,512,256]{2,1,0:T(8,128)(2,1)S(1)}, u32[]{:S(2)}, u32[]{:S(2)}) collective-permute-start(bf16[2,512,256]{2,1,0:T(8,128)(2,1)S(1)} %collective-permute-done.3), channel_id=1, source_target_pairs={{0,2},{2,0},{8,10},{10,8},{16,18},{18,16},{24,26},{26,24},{28,30},... | collective-permute-start | bytes 1572872 | tf_op jit(solution)/shard_map/ppermute | solution.py:370
  54.4 9.2 %collective-permute-start.5 = (bf16[2,512,256]{2,1,0:T(8,128)(2,1)S(1)}, bf16[2,512,256]{2,1,0:T(8,128)(2,1)S(1)}, u32[]{:S(2)}, u32[]{:S(2)}) collective-permute-start(bf16[2,512,256]{2,1,0:T(8,128)(2,1)S(1)} %collective-permute-done.3), channel_id=1, source_target_pairs={{0,8},{8,16},{16,24},{24,28},{28,20},{20,12},{12,4},{4,0},{2,6},{1... | collective-permute-start | bytes 1572872 | tf_op jit(solution)/shard_map/ppermute | solution.py:368
  58.0 13.0 %collective-permute-start.17 = (bf16[2,512,256]{2,1,0:T(8,128)(2,1)S(1)}, bf16[2,512,256]{2,1,0:T(8,128)(2,1)S(1)}, u32[]{:S(2)}, u32[]{:S(2)}) collective-permute-start(bf16[2,512,256]{2,1,0:T(8,128)(2,1)S(1)} %collective-permute-done.15), channel_id=1, source_target_pairs={{0,2},{2,0},{8,10},{10,8},{16,18},{18,16},{24,26},{26,24},{28,30},... | collective-permute-start | bytes 1572872 | tf_op jit(solution)/shard_map/ppermute | solution.py:370
  60.0 6.7 %collective-permute-start.18 = (bf16[1,512,256]{2,1,0:T(8,128)(2,1)S(1)}, bf16[1,512,256]{2,1,0:T(8,128)(2,1)S(1)}, u32[]{:S(2)}, u32[]{:S(2)}) collective-permute-start(bf16[1,512,256]{2,1,0:T(8,128)(2,1)S(1)} %slice.7), channel_id=1, source_target_pairs={{0,8},{8,16},{16,24},{24,28},{28,20},{20,12},{12,4},{4,0},{2,6},{1... | collective-permute-start | bytes 786440 | tf_op jit(solution)/shard_map/ppermute | solution.py:368
  63.6 5.7 %collective-permute-start.8 = (bf16[1,512,256]{2,1,0:T(8,128)(2,1)S(1)}, bf16[1,512,256]{2,1,0:T(8,128)(2,1)S(1)}, u32[]{:S(2)}, u32[]{:S(2)}) collective-permute-start(bf16[1,512,256]{2,1,0:T(8,128)(2,1)S(1)} %slice.6), channel_id=1, source_target_pairs={{0,8},{8,16},{16,24},{24,28},{28,20},{20,12},{12,4},{4,0},{2,6},{1... | collective-permute-start | bytes 786440 | tf_op jit(solution)/shard_map/ppermute | solution.py:368
  65.0 7.9 %collective-permute-start.7 = (bf16[2,512,256]{2,1,0:T(8,128)(2,1)S(1)}, bf16[2,512,256]{2,1,0:T(8,128)(2,1)S(1)}, u32[]{:S(2)}, u32[]{:S(2)}) collective-permute-start(bf16[2,512,256]{2,1,0:T(8,128)(2,1)S(1)} %collective-permute-done.5), channel_id=1, source_target_pairs={{0,2},{2,0},{8,10},{10,8},{16,18},{18,16},{24,26},{26,24},{28,30},... | collective-permute-start | bytes 1572872 | tf_op jit(solution)/shard_map/ppermute | solution.py:370
  66.7 5.3 %collective-permute-start.19 = (bf16[1,512,256]{2,1,0:T(8,128)(2,1)S(1)}, bf16[1,512,256]{2,1,0:T(8,128)(2,1)S(1)}, u32[]{:S(2)}, u32[]{:S(2)}) collective-permute-start(bf16[1,512,256]{2,1,0:T(8,128)(2,1)S(1)} %collective-permute-done.18), channel_id=1, source_target_pairs={{0,2},{2,0},{8,10},{10,8},{16,18},{18,16},{24,26},{26,24},{28,30},... | collective-permute-start | bytes 786440 | tf_op jit(solution)/shard_map/ppermute | solution.py:370
  69.3 4.7 %collective-permute-start.9 = (bf16[1,512,256]{2,1,0:T(8,128)(2,1)S(1)}, bf16[1,512,256]{2,1,0:T(8,128)(2,1)S(1)}, u32[]{:S(2)}, u32[]{:S(2)}) collective-permute-start(bf16[1,512,256]{2,1,0:T(8,128)(2,1)S(1)} %collective-permute-done.8), channel_id=1, source_target_pairs={{0,2},{2,0},{8,10},{10,8},{16,18},{18,16},{24,26},{26,24},{28,30},... | collective-permute-start | bytes 786440 | tf_op jit(solution)/shard_map/ppermute | solution.py:370
  74.8 24.0 %copy-start.1 = (bf16[64,4,4096]{2,1,0:T(4,128)(2,1)S(1)}, bf16[64,4,4096]{2,1,0:T(4,128)(2,1)}, u32[]{:S(2)}) copy-start(bf16[64,4,4096]{2,1,0:T(4,128)(2,1)} %param.8) | copy-start | bytes 6291460

commit v3 on v2

--- a/solution.py
+++ b/solution.py
@@ -354,7 +354,7 @@
 def gather_blocks(chunks, swap, ring):
     move = functools.partial(lax.ppermute, axis_name="chan")
     count = len(ring)
-    current = [jnp.concatenate([own, move(own, perm=swap)], axis=0) for own in chunks]
+    current = [lax.optimization_barrier(jnp.concatenate([own, move(own, perm=swap)], axis=0)) for own in chunks]
     gathered = [reserve((count,) + own.shape[1:]) for own in chunks]
 
     def put(k, pieces, slot):

time: 99 us -> 98.4 us (level)
  waiting for transfers between devices: 20.5 us -> 18.5 us
  local copies, waits for them, and re-layouts: 4.51 us -> 6.17 us
    ppermute x8, waiting for transfers between devices: 14.2 us -> 12.2 us  [gather_blocks(): move(current[k][:1] if step == steps else current[k], perm=ring)]
    dynamic_update_slice x0 -> x2, local copies, waits for them, and re-layouts: none -> 1.67 us  [put(): gathered[k] = lax.dynamic_update_slice(gathered[k], piece, (slot, 0, 0))]
    dynamic_update_slice x10 -> x8, other arithmetic: 9.92 us -> 9.11 us  [put(): gathered[k] = lax.dynamic_update_slice(gathered[k], piece, (slot, 0, 0))]
  transfers between devices with their start and end apart: 20 -> 20, of which waited for: 7 -> 7; matrix products, arithmetic and copies ran while one was open for 11% -> 12% of each run, Pallas kernels for 10% -> 10%
where the time goes in v3:
time: 98.4 us; the launch traced here: 98 us
  Pallas kernels  35.7 us (36%)
  starting transfers between devices  27.4 us (28%)
  waiting for transfers between devices  18.5 us (19%)
  other arithmetic  10 us (10%)
  local copies, waits for them, and re-layouts  6.17 us (6%)
    pallas_call x1, Pallas kernels, cross_spectra(): pl.pallas_call(cross_kernel, in_specs=[smem, smem] + [hbm] * len(gathered...  24 us
    ppermute x8, starting transfers between devices, gather_blocks(): move(current[k][:1] if step == steps else current[k], perm=ring)  12.6 us
    ppermute x8, waiting for transfers between devices, gather_blocks(): move(current[k][:1] if step == steps else current[k], perm=ring)  12.2 us
    ppermute x8, starting transfers between devices, gather_blocks(): waiting[k] = ([current[k], move(current[k], perm=swap)], 4 * step - 2)  10.3 us
    pallas_call x2, Pallas kernels, whiten(): pl.pallas_call(whiten_kernel, in_specs=[pl.BlockSpec(memory_space=pltpu.S...  9.82 us
    dynamic_update_slice x8, other arithmetic, put(): gathered[k] = lax.dynamic_update_slice(gathered[k], piece, (slot, 0, 0))  9.11 us
    ppermute x2, waiting for transfers between devices, body(): lax.ppermute(message, 'band', [(0, 1), (1, 0)])  6.31 us
    ppermute x2, starting transfers between devices, gather_blocks(): move(own, perm=swap)  2.34 us
  transfers between devices with their start and end apart: 20, of which 7 were waited for; matrix products, arithmetic and copies ran while one was open for 12% of the time, Pallas kernels for 10%

profile of v3, /device:TPU:1, one launch (start us, length us, event | category | flops | bytes accessed | tf_op | source)
XLA Modules:
  0.0 98.0 jit_solution(14200480378698846468)
XLA Ops:
  0.0 0.0 copy-start.2
  0.0 0.8 pad_clamp_fusion
  0.8 0.8 copy-done
  1.6 1.4 %gather_fusion = bf16[32,4,4096]{2,1,0:T(4,128)(2,1)S(1)} fusion(bf16[64,4,4096]{2,1,0:T(4,128)(2,1)S(1)} %copy-done, s32[1024]{0:T(1024)S(1)} %pad_clamp_fusion), kind=kCustom, calls=%fused_computation | custom fusion | bytes 2097280 | tf_op jit(solution)/shard_map/gather | solution.py:415
  3.1 0.3 reshape.13.raw_ref
  3.3 0.0 copy-done.3
  3.4 1.9 %decimate.1 = (bf16[64,2176]{1,0:T(8,128)(2,1)S(1)}, bf16[64,2176]{1,0:T(8,128)(2,1)S(1)}) custom-call(bf16[128,128]{1,0:T(8,128)(2,1)S(1)} %copy-done.4, bf16[128,4096]{1,0:T(8,128)(2,1)S(1)} %reshape.13.raw_ref, bf16[384,256]{1,0:T(8,128)(2,1)S(1)} %copy-done.3), custom_call_target="tpu_custom_call" | custom-call | tf_op jit(solution)/shard_map/decimate/pallas_call | solution.py:417
  5.3 2.1 %collective-permute-start.10 = (bf16[64,2176]{1,0:T(8,128)(2,1)S(1)}, bf16[64,2176]{1,0:T(8,128)(2,1)S(1)}, u32[]{:S(2)}, u32[]{:S(2)}) collective-permute-start(bf16[64,2176]{1,0:T(8,128)(2,1)S(1)} %get-tuple-element.26.own_ref), channel_id=1, source_target_pairs={{0,1},{1,0},{2,3},{3,2},{4,5},{5,4},{6,7},{7,6},{8,9},{9,8},{10,11... | collective-permute-start | bytes 835592 | tf_op jit(solution)/shard_map/ppermute | solution.py:423
  7.4 0.1 collective-permute-start
  7.5 6.3 %collective-permute-done.10.other_ref = bf16[64,2176]{1,0:T(8,128)(2,1)S(1)} collective-permute-done((bf16[64,2176]{1,0:T(8,128)(2,1)S(1)}, bf16[64,2176]{1,0:T(8,128)(2,1)S(1)}, u32[]{:S(2)}, u32[]{:S(2)}) %collective-permute-start.10) | collective-permute-done | bytes 278560 | tf_op jit(solution)/shard_map/ppermute | solution.py:423
  13.8 4.9 %whiten.3 = bf16[1,512,256]{2,1,0:T(8,128)(2,1)S(1)} custom-call(s32[1]{0:T(128)} %bitcast.1.band_ref, bf16[64,2176]{1,0:T(8,128)(2,1)S(1)} %get-tuple-element.26.own_ref, bf16[64,2176]{1,0:T(8,128)(2,1)S(1)} %collective-permute-done.10.other_ref, bf16[128,256]{1,0:T(8,128)(2,1)S(1)} %copy-done.2, bf16[2,9,2048,256]{3,2,1,0:T(8,128)(2,1)} %constant.30.clone.table_ref), custom_call_target="tpu_custom_call" | custom-call | bytes 40000000 | tf_op jit(solution)/shard_map/whiten/pallas_call | solution.py:427
  18.7 2.1 %collective-permute-start.11 = (bf16[1,512,256]{2,1,0:T(8,128)(2,1)S(1)}, bf16[1,512,256]{2,1,0:T(8,128)(2,1)S(1)}, u32[]{:S(2)}, u32[]{:S(2)}) collective-permute-start(bf16[1,512,256]{2,1,0:T(8,128)(2,1)S(1)} %whiten.3), channel_id=1, source_target_pairs={{0,2},{2,0},{8,10},{10,8},{16,18},{18,16},{24,26},{26,24},{28,30},... | collective-permute-start | bytes 786440 | tf_op jit(solution)/shard_map/ppermute | solution.py:357
  20.8 0.0 collective-permute-done.other_ref
  20.8 4.9 %whiten.2 = bf16[1,512,256]{2,1,0:T(8,128)(2,1)S(1)} custom-call(s32[1]{0:T(128)} %bitcast.1.band_ref, bf16[64,2176]{1,0:T(8,128)(2,1)S(1)} %get-tuple-element.19.own_ref, bf16[64,2176]{1,0:T(8,128)(2,1)S(1)} %collective-permute-done.other_ref, bf16[128,256]{1,0:T(8,128)(2,1)S(1)} %copy-done.2, bf16[2,9,2048,256]{3,2,1,0:T(8,128)(2,1)} %constant.30.clone.table_ref), custom_call_target="tpu_custom_call" | custom-call | bytes 40000000 | tf_op jit(solution)/shard_map/whiten/pallas_call | solution.py:427
  25.8 0.2 collective-permute-start.1
  26.0 0.0 collective-permute-done.11
  26.0 0.1 pad_maximum_fusion.1
  26.0 1.7 %collective-permute-start.12 = (bf16[2,512,256]{2,1,0:T(8,128)(2,1)S(1)}, bf16[2,512,256]{2,1,0:T(8,128)(2,1)}, u32[]{:S(2)}, u32[]{:S(2)}) collective-permute-start(bf16[2,512,256]{2,1,0:T(8,128)(2,1)S(1)} %pad_maximum_fusion.1), channel_id=1, source_target_pairs={{0,8},{8,16},{16,24},{24,28},{28,20},{20,12},{12,4},{4,0},{2,6},{1... | collective-permute-start | bytes 1572872 | tf_op jit(solution)/shard_map/ppermute | solution.py:368
  27.7 0.0 collective-permute-done.1
  27.7 0.1 pad_maximum_fusion
  27.8 1.4 %collective-permute-start.2 = (bf16[2,512,256]{2,1,0:T(8,128)(2,1)S(1)}, bf16[2,512,256]{2,1,0:T(8,128)(2,1)S(1)}, u32[]{:S(2)}, u32[]{:S(2)}) collective-permute-start(bf16[2,512,256]{2,1,0:T(8,128)(2,1)S(1)} %pad_maximum_fusion), channel_id=1, source_target_pairs={{0,8},{8,16},{16,24},{24,28},{28,20},{20,12},{12,4},{4,0},{2,6},{1... | collective-permute-start | bytes 1572872 | tf_op jit(solution)/shard_map/ppermute | solution.py:368
  29.2 5.6 %collective-permute-done.12 = bf16[2,512,256]{2,1,0:T(8,128)(2,1)} collective-permute-done((bf16[2,512,256]{2,1,0:T(8,128)(2,1)S(1)}, bf16[2,512,256]{2,1,0:T(8,128)(2,1)}, u32[]{:S(2)}, u32[]{:S(2)}) %collective-permute-start.12) | collective-permute-done | bytes 524320 | tf_op jit(solution)/shard_map/ppermute | solution.py:368
  34.8 1.0 collective-permute-start.14
  35.7 0.8 constant_dynamic-update-slice_fusion
  36.6 1.7 %collective-permute-start.13 = (bf16[2,512,256]{2,1,0:T(8,128)(2,1)}, bf16[2,512,256]{2,1,0:T(8,128)(2,1)S(1)}, u32[]{:S(2)}, u32[]{:S(2)}) collective-permute-start(bf16[2,512,256]{2,1,0:T(8,128)(2,1)} %collective-permute-done.12), channel_id=1, source_target_pairs={{0,8},{8,16},{16,24},{24,28},{28,20},{20,12},{12,4},{4,0},{2,6},{1... | collective-permute-start | bytes 1572872 | tf_op jit(solution)/shard_map/ppermute | solution.py:368
  38.3 0.8 constant_dynamic-update-slice_fusion.1
  39.2 1.1 %collective-permute-done.2 = bf16[2,512,256]{2,1,0:T(8,128)(2,1)S(1)} collective-permute-done((bf16[2,512,256]{2,1,0:T(8,128)(2,1)S(1)}, bf16[2,512,256]{2,1,0:T(8,128)(2,1)S(1)}, u32[]{:S(2)}, u32[]{:S(2)}) %collective-permute-start.2) | collective-permute-done | bytes 524320 | tf_op jit(solution)/shard_map/ppermute | solution.py:368
  40.3 1.4 %collective-permute-start.3 = (bf16[2,512,256]{2,1,0:T(8,128)(2,1)S(1)}, bf16[2,512,256]{2,1,0:T(8,128)(2,1)S(1)}, u32[]{:S(2)}, u32[]{:S(2)}) collective-permute-start(bf16[2,512,256]{2,1,0:T(8,128)(2,1)S(1)} %collective-permute-done.2), channel_id=1, source_target_pairs={{0,8},{8,16},{16,24},{24,28},{28,20},{20,12},{12,4},{4,0},{2,6},{1... | collective-permute-start | bytes 1572872 | tf_op jit(solution)/shard_map/ppermute | solution.py:368
  41.7 1.7 %collective-permute-start.4 = (bf16[2,512,256]{2,1,0:T(8,128)(2,1)S(1)}, bf16[2,512,256]{2,1,0:T(8,128)(2,1)S(1)}, u32[]{:S(2)}, u32[]{:S(2)}) collective-permute-start(bf16[2,512,256]{2,1,0:T(8,128)(2,1)S(1)} %collective-permute-done.2), channel_id=1, source_target_pairs={{0,2},{2,0},{8,10},{10,8},{16,18},{18,16},{24,26},{26,24},{28,30},... | collective-permute-start | bytes 1572872 | tf_op jit(solution)/shard_map/ppermute | solution.py:370
  43.4 0.0 collective-permute-done.14
  43.4 2.1 %maximum_dynamic-update-slice_fusion.3 = bf16[16,512,256]{2,1,0:T(8,128)(2,1)} fusion(bf16[16,512,256]{2,1,0:T(8,128)(2,1)} %constant_dynamic-update-slice_fusion, bf16[2,512,256]{2,1,0:T(8,128)(2,1)S(1)} %collective-permute-done.14, bf16[2,512,256]{2,1,0:T(8,128)(2,1)} %collective-permute-done.12), kind=kLoop, calls=%fused_computation.4 | loop fusion | flops 2097152 | bytes 2097152 | tf_op jit(solution)/shard_map/dynamic_update_slice | solution.py:362
  45.5 0.4 collective-permute-done.13
  45.9 1.4 %collective-permute-start.15 = (bf16[2,512,256]{2,1,0:T(8,128)(2,1)S(1)}, bf16[2,512,256]{2,1,0:T(8,128)(2,1)S(1)}, u32[]{:S(2)}, u32[]{:S(2)}) collective-permute-start(bf16[2,512,256]{2,1,0:T(8,128)(2,1)S(1)} %collective-permute-done.13), channel_id=1, source_target_pairs={{0,8},{8,16},{16,24},{24,28},{28,20},{20,12},{12,4},{4,0},{2,6},{1... | collective-permute-start | bytes 1572872 | tf_op jit(solution)/shard_map/ppermute | solution.py:368
  47.3 1.7 %collective-permute-start.16 = (bf16[2,512,256]{2,1,0:T(8,128)(2,1)S(1)}, bf16[2,512,256]{2,1,0:T(8,128)(2,1)S(1)}, u32[]{:S(2)}, u32[]{:S(2)}) collective-permute-start(bf16[2,512,256]{2,1,0:T(8,128)(2,1)S(1)} %collective-permute-done.13), channel_id=1, source_target_pairs={{0,2},{2,0},{8,10},{10,8},{16,18},{18,16},{24,26},{26,24},{28,30},... | collective-permute-start | bytes 1572872 | tf_op jit(solution)/shard_map/ppermute | solution.py:370
  49.0 2.5 %collective-permute-done.3 = bf16[2,512,256]{2,1,0:T(8,128)(2,1)S(1)} collective-permute-done((bf16[2,512,256]{2,1,0:T(8,128)(2,1)S(1)}, bf16[2,512,256]{2,1,0:T(8,128)(2,1)S(1)}, u32[]{:S(2)}, u32[]{:S(2)}) %collective-permute-start.3) | collective-permute-done | bytes 524320 | tf_op jit(solution)/shard_map/ppermute | solution.py:368
  51.5 1.0 collective-permute-start.6
  52.5 0.0 collective-permute-done.4
  52.5 1.1 %maximum_dynamic-update-slice_fusion = bf16[16,512,256]{2,1,0:T(8,128)(2,1)} fusion(bf16[16,512,256]{2,1,0:T(8,128)(2,1)} %constant_dynamic-update-slice_fusion.1, bf16[2,512,256]{2,1,0:T(8,128)(2,1)S(1)} %collective-permute-done.4, bf16[2,512,256]{2,1,0:T(8,128)(2,1)S(1)} %collective-permute-done.2), kind=kLoop, calls=%fused_computation.1 | loop fusion | flops 2097152 | bytes 2097152 | tf_op jit(solution)/shard_map/dynamic_update_slice | solution.py:362
  53.6 1.7 %collective-permute-start.5 = (bf16[2,512,256]{2,1,0:T(8,128)(2,1)S(1)}, bf16[2,512,256]{2,1,0:T(8,128)(2,1)S(1)}, u32[]{:S(2)}, u32[]{:S(2)}) collective-permute-start(bf16[2,512,256]{2,1,0:T(8,128)(2,1)S(1)} %collective-permute-done.3), channel_id=1, source_target_pairs={{0,8},{8,16},{16,24},{24,28},{28,20},{20,12},{12,4},{4,0},{2,6},{1... | collective-permute-start | bytes 1572872 | tf_op jit(solution)/shard_map/ppermute | solution.py:368
  55.3 1.8 %collective-permute-done.15 = bf16[2,512,256]{2,1,0:T(8,128)(2,1)S(1)} collective-permute-done((bf16[2,512,256]{2,1,0:T(8,128)(2,1)S(1)}, bf16[2,512,256]{2,1,0:T(8,128)(2,1)S(1)}, u32[]{:S(2)}, u32[]{:S(2)}) %collective-permute-start.15) | collective-permute-done | bytes 524320 | tf_op jit(solution)/shard_map/ppermute | solution.py:368
  57.1 1.0 collective-permute-start.17
  58.1 0.0 collective-permute-done.16
  58.1 1.1 %maximum_dynamic-update-slice_fusion.4 = bf16[16,512,256]{2,1,0:T(8,128)(2,1)} fusion(bf16[16,512,256]{2,1,0:T(8,128)(2,1)} %maximum_dynamic-update-slice_fusion.3, bf16[2,512,256]{2,1,0:T(8,128)(2,1)S(1)} %collective-permute-done.16, bf16[2,512,256]{2,1,0:T(8,128)(2,1)S(1)} %collective-permute-done.13), kind=kLoop, calls=%fused_computation.5 | loop fusion | flops 2097152 | bytes 2097152 | tf_op jit(solution)/shard_map/dynamic_update_slice | solution.py:362
  59.2 1.8 %collective-permute-start.18 = (bf16[1,512,256]{2,1,0:T(8,128)(2,1)S(1)}, bf16[1,512,256]{2,1,0:T(8,128)(2,1)S(1)}, u32[]{:S(2)}, u32[]{:S(2)}) collective-permute-start(bf16[1,512,256]{2,1,0:T(8,128)(2,1)S(1)} %slice.7), channel_id=1, source_target_pairs={{0,8},{8,16},{16,24},{24,28},{28,20},{20,12},{12,4},{4,0},{2,6},{1... | collective-permute-start | bytes 786440 | tf_op jit(solution)/shard_map/ppermute | solution.py:368
  61.0 0.0 collective-permute-done.6
  61.0 1.0 %maximum_dynamic-update-slice_fusion.1 = bf16[16,512,256]{2,1,0:T(8,128)(2,1)} fusion(bf16[16,512,256]{2,1,0:T(8,128)(2,1)} %maximum_dynamic-update-slice_fusion, bf16[2,512,256]{2,1,0:T(8,128)(2,1)S(1)} %collective-permute-done.6, bf16[2,512,256]{2,1,0:T(8,128)(2,1)S(1)} %collective-permute-done.3), kind=kLoop, calls=%fused_computation.2 | loop fusion | flops 2097152 | bytes 2097152 | tf_op jit(solution)/shard_map/dynamic_update_slice | solution.py:362
  62.0 0.7 collective-permute-done.5
  62.8 1.4 %collective-permute-start.8 = (bf16[1,512,256]{2,1,0:T(8,128)(2,1)S(1)}, bf16[1,512,256]{2,1,0:T(8,128)(2,1)S(1)}, u32[]{:S(2)}, u32[]{:S(2)}) collective-permute-start(bf16[1,512,256]{2,1,0:T(8,128)(2,1)S(1)} %slice.6), channel_id=1, source_target_pairs={{0,8},{8,16},{16,24},{24,28},{28,20},{20,12},{12,4},{4,0},{2,6},{1... | collective-permute-start | bytes 786440 | tf_op jit(solution)/shard_map/ppermute | solution.py:368
  64.2 1.7 %collective-permute-start.7 = (bf16[2,512,256]{2,1,0:T(8,128)(2,1)S(1)}, bf16[2,512,256]{2,1,0:T(8,128)(2,1)S(1)}, u32[]{:S(2)}, u32[]{:S(2)}) collective-permute-start(bf16[2,512,256]{2,1,0:T(8,128)(2,1)S(1)} %collective-permute-done.5), channel_id=1, source_target_pairs={{0,2},{2,0},{8,10},{10,8},{16,18},{18,16},{24,26},{26,24},{28,30},... | collective-permute-start | bytes 1572872 | tf_op jit(solution)/shard_map/ppermute | solution.py:370
  65.9 0.0 collective-permute-done.18
  65.9 0.6 collective-permute-start.19
  66.5 0.7 copy.9.pairs_ref
  67.2 1.3 %fusion.slot_ref = s32[16]{0:T(128)} fusion(s32[16,16]{1,0:T(8,128)} %constant.34.clone, s32[]{:T(128)S(6)} %select_n.3), kind=kLoop, calls=%fused_computation.15 | loop fusion | bytes 132 | tf_op jit(solution)/shard_map/squeeze | solution.py:450
  68.5 0.0 collective-permute-done.8
  68.5 1.7 %collective-permute-start.9 = (bf16[1,512,256]{2,1,0:T(8,128)(2,1)S(1)}, bf16[1,512,256]{2,1,0:T(8,128)(2,1)S(1)}, u32[]{:S(2)}, u32[]{:S(2)}) collective-permute-start(bf16[1,512,256]{2,1,0:T(8,128)(2,1)S(1)} %collective-permute-done.8), channel_id=1, source_target_pairs={{0,2},{2,0},{8,10},{10,8},{16,18},{18,16},{24,26},{26,24},{28,30},... | collective-permute-start | bytes 786440 | tf_op jit(solution)/shard_map/ppermute | solution.py:370
  70.2 0.0 collective-permute-done.17
  70.2 1.1 %maximum_dynamic-update-slice_fusion.5 = bf16[16,512,256]{2,1,0:T(8,128)(2,1)} fusion(bf16[16,512,256]{2,1,0:T(8,128)(2,1)} %maximum_dynamic-update-slice_fusion.4, bf16[2,512,256]{2,1,0:T(8,128)(2,1)S(1)} %collective-permute-done.17, bf16[2,512,256]{2,1,0:T(8,128)(2,1)S(1)} %collective-permute-done.15), kind=kLoop, calls=%fused_computation.6 | loop fusion | flops 2097152 | bytes 2097152 | tf_op jit(solution)/shard_map/dynamic_update_slice | solution.py:362
  71.2 0.0 collective-permute-done.19
  71.2 0.9 maximum_dynamic-update-slice_fusion.7.refs_1_
  72.1 0.0 collective-permute-done.7
  72.1 1.0 %maximum_dynamic-update-slice_fusion.2 = bf16[16,512,256]{2,1,0:T(8,128)(2,1)} fusion(bf16[16,512,256]{2,1,0:T(8,128)(2,1)} %maximum_dynamic-update-slice_fusion.1, bf16[2,512,256]{2,1,0:T(8,128)(2,1)S(1)} %collective-permute-done.7, bf16[2,512,256]{2,1,0:T(8,128)(2,1)S(1)} %collective-permute-done.5), kind=kLoop, calls=%fused_computation.3 | loop fusion | flops 2097152 | bytes 2097152 | tf_op jit(solution)/shard_map/dynamic_update_slice | solution.py:362
  73.2 0.0 collective-permute-done.9
  73.2 0.8 maximum_dynamic-update-slice_fusion.6.refs_0_
  74.0 24.0 %cross_spectra.1 = bf16[8,32,32,16,128]{4,3,2,1,0:T(8,128)(2,1)} custom-call(s32[8,2]{1,0:T(8,128)} %copy.9.pairs_ref, s32[16]{0:T(128)} %fusion.slot_ref, bf16[16,512,256]{2,1,0:T(8,128)(2,1)} %maximum_dynamic-update-slice_fusion.6.refs_0_, bf16[16,512,256]{2,1,0:T(8,128)(2,1)} %maximum_dynamic-update-slice_fusion.7.refs_1_), custom_call_target="tpu_custom_call" | custom-call | tf_op jit(solution)/shard_map/cross_spectra/pallas_call | solution.py:319
  (13 shorter events, 0.1 us)
Async XLA Ops:
  0.0 1.6 %copy-start = (bf16[64,4,4096]{2,1,0:T(4,128)(2,1)S(1)}, bf16[64,4,4096]{2,1,0:T(4,128)(2,1)}, u32[]{:S(2)}) copy-start(bf16[64,4,4096]{2,1,0:T(4,128)(2,1)} %param.8) | copy-start | bytes 6291460
  0.0 3.3 %copy-start.3 = (bf16[384,256]{1,0:T(8,128)(2,1)S(1)}, bf16[384,256]{1,0:T(8,128)(2,1)}, u32[]{:S(2)}) copy-start(bf16[384,256]{1,0:T(8,128)(2,1)} %constant.32.clone.inner_ref) | copy-start | bytes 589828
  0.0 3.4 %copy-start.4 = (bf16[128,128]{1,0:T(8,128)(2,1)S(1)}, bf16[128,128]{1,0:T(8,128)(2,1)}, u32[]{:S(2)}) copy-start(bf16[128,128]{1,0:T(8,128)(2,1)} %constant.31.clone.order_ref) | copy-start | bytes 98308
  0.0 13.8 %copy-start.2 = (bf16[128,256]{1,0:T(8,128)(2,1)S(1)}, bf16[128,256]{1,0:T(8,128)(2,1)}, u32[]{:S(2)}) copy-start(bf16[128,256]{1,0:T(8,128)(2,1)} %constant.33.clone.first_ref) | copy-start | bytes 196612
  5.3 8.5 %collective-permute-start.10 = (bf16[64,2176]{1,0:T(8,128)(2,1)S(1)}, bf16[64,2176]{1,0:T(8,128)(2,1)S(1)}, u32[]{:S(2)}, u32[]{:S(2)}) collective-permute-start(bf16[64,2176]{1,0:T(8,128)(2,1)S(1)} %get-tuple-element.26.own_ref), channel_id=1, source_target_pairs={{0,1},{1,0},{2,3},{3,2},{4,5},{5,4},{6,7},{7,6},{8,9},{9,8},{10,11... | collective-permute-start | bytes 835592 | tf_op jit(solution)/shard_map/ppermute | solution.py:423
  7.4 13.4 %collective-permute-start = (bf16[64,2176]{1,0:T(8,128)(2,1)S(1)}, bf16[64,2176]{1,0:T(8,128)(2,1)S(1)}, u32[]{:S(2)}, u32[]{:S(2)}) collective-permute-start(bf16[64,2176]{1,0:T(8,128)(2,1)S(1)} %get-tuple-element.19.own_ref), channel_id=1, source_target_pairs={{0,1},{1,0},{2,3},{3,2},{4,5},{5,4},{6,7},{7,6},{8,9},{9,8},{10,11... | collective-permute-start | bytes 835592 | tf_op jit(solution)/shard_map/ppermute | solution.py:423
  18.7 7.3 %collective-permute-start.11 = (bf16[1,512,256]{2,1,0:T(8,128)(2,1)S(1)}, bf16[1,512,256]{2,1,0:T(8,128)(2,1)S(1)}, u32[]{:S(2)}, u32[]{:S(2)}) collective-permute-start(bf16[1,512,256]{2,1,0:T(8,128)(2,1)S(1)} %whiten.3), channel_id=1, source_target_pairs={{0,2},{2,0},{8,10},{10,8},{16,18},{18,16},{24,26},{26,24},{28,30},... | collective-permute-start | bytes 786440 | tf_op jit(solution)/shard_map/ppermute | solution.py:357
  25.8 2.0 %collective-permute-start.1 = (bf16[1,512,256]{2,1,0:T(8,128)(2,1)S(1)}, bf16[1,512,256]{2,1,0:T(8,128)(2,1)S(1)}, u32[]{:S(2)}, u32[]{:S(2)}) collective-permute-start(bf16[1,512,256]{2,1,0:T(8,128)(2,1)S(1)} %whiten.2), channel_id=1, source_target_pairs={{0,2},{2,0},{8,10},{10,8},{16,18},{18,16},{24,26},{26,24},{28,30},... | collective-permute-start | bytes 786440 | tf_op jit(solution)/shard_map/ppermute | solution.py:357
  26.0 8.7 %collective-permute-start.12 = (bf16[2,512,256]{2,1,0:T(8,128)(2,1)S(1)}, bf16[2,512,256]{2,1,0:T(8,128)(2,1)}, u32[]{:S(2)}, u32[]{:S(2)}) collective-permute-start(bf16[2,512,256]{2,1,0:T(8,128)(2,1)S(1)} %pad_maximum_fusion.1), channel_id=1, source_target_pairs={{0,8},{8,16},{16,24},{24,28},{28,20},{20,12},{12,4},{4,0},{2,6},{1... | collective-permute-start | bytes 1572872 | tf_op jit(solution)/shard_map/ppermute | solution.py:368
  27.8 12.5 %collective-permute-start.2 = (bf16[2,512,256]{2,1,0:T(8,128)(2,1)S(1)}, bf16[2,512,256]{2,1,0:T(8,128)(2,1)S(1)}, u32[]{:S(2)}, u32[]{:S(2)}) collective-permute-start(bf16[2,512,256]{2,1,0:T(8,128)(2,1)S(1)} %pad_maximum_fusion), channel_id=1, source_target_pairs={{0,8},{8,16},{16,24},{24,28},{28,20},{20,12},{12,4},{4,0},{2,6},{1... | collective-permute-start | bytes 1572872 | tf_op jit(solution)/shard_map/ppermute | solution.py:368
  34.8 8.6 %collective-permute-start.14 = (bf16[2,512,256]{2,1,0:T(8,128)(2,1)}, bf16[2,512,256]{2,1,0:T(8,128)(2,1)S(1)}, u32[]{:S(2)}, u32[]{:S(2)}) collective-permute-start(bf16[2,512,256]{2,1,0:T(8,128)(2,1)} %collective-permute-done.12), channel_id=1, source_target_pairs={{0,2},{2,0},{8,10},{10,8},{16,18},{18,16},{24,26},{26,24},{28,30},... | collective-permute-start | bytes 1572872 | tf_op jit(solution)/shard_map/ppermute | solution.py:370
  36.6 9.3 %collective-permute-start.13 = (bf16[2,512,256]{2,1,0:T(8,128)(2,1)}, bf16[2,512,256]{2,1,0:T(8,128)(2,1)S(1)}, u32[]{:S(2)}, u32[]{:S(2)}) collective-permute-start(bf16[2,512,256]{2,1,0:T(8,128)(2,1)} %collective-permute-done.12), channel_id=1, source_target_pairs={{0,8},{8,16},{16,24},{24,28},{28,20},{20,12},{12,4},{4,0},{2,6},{1... | collective-permute-start | bytes 1572872 | tf_op jit(solution)/shard_map/ppermute | solution.py:368
  40.3 11.2 %collective-permute-start.3 = (bf16[2,512,256]{2,1,0:T(8,128)(2,1)S(1)}, bf16[2,512,256]{2,1,0:T(8,128)(2,1)S(1)}, u32[]{:S(2)}, u32[]{:S(2)}) collective-permute-start(bf16[2,512,256]{2,1,0:T(8,128)(2,1)S(1)} %collective-permute-done.2), channel_id=1, source_target_pairs={{0,8},{8,16},{16,24},{24,28},{28,20},{20,12},{12,4},{4,0},{2,6},{1... | collective-permute-start | bytes 1572872 | tf_op jit(solution)/shard_map/ppermute | solution.py:368
  41.7 10.8 %collective-permute-start.4 = (bf16[2,512,256]{2,1,0:T(8,128)(2,1)S(1)}, bf16[2,512,256]{2,1,0:T(8,128)(2,1)S(1)}, u32[]{:S(2)}, u32[]{:S(2)}) collective-permute-start(bf16[2,512,256]{2,1,0:T(8,128)(2,1)S(1)} %collective-permute-done.2), channel_id=1, source_target_pairs={{0,2},{2,0},{8,10},{10,8},{16,18},{18,16},{24,26},{26,24},{28,30},... | collective-permute-start | bytes 1572872 | tf_op jit(solution)/shard_map/ppermute | solution.py:370
  45.5 21.1 %copy-start.5 = (s32[8,2]{0,1:T(2,128)S(1)}, s32[8,2]{0,1:T(2,128)}, u32[]{:S(2)}) copy-start(s32[8,2]{0,1:T(2,128)} %param.10) | copy-start | bytes 196
  45.9 11.2 %collective-permute-start.15 = (bf16[2,512,256]{2,1,0:T(8,128)(2,1)S(1)}, bf16[2,512,256]{2,1,0:T(8,128)(2,1)S(1)}, u32[]{:S(2)}, u32[]{:S(2)}) collective-permute-start(bf16[2,512,256]{2,1,0:T(8,128)(2,1)S(1)} %collective-permute-done.13), channel_id=1, source_target_pairs={{0,8},{8,16},{16,24},{24,28},{28,20},{20,12},{12,4},{4,0},{2,6},{1... | collective-permute-start | bytes 1572872 | tf_op jit(solution)/shard_map/ppermute | solution.py:368
  47.3 10.8 %collective-permute-start.16 = (bf16[2,512,256]{2,1,0:T(8,128)(2,1)S(1)}, bf16[2,512,256]{2,1,0:T(8,128)(2,1)S(1)}, u32[]{:S(2)}, u32[]{:S(2)}) collective-permute-start(bf16[2,512,256]{2,1,0:T(8,128)(2,1)S(1)} %collective-permute-done.13), channel_id=1, source_target_pairs={{0,2},{2,0},{8,10},{10,8},{16,18},{18,16},{24,26},{26,24},{28,30},... | collective-permute-start | bytes 1572872 | tf_op jit(solution)/shard_map/ppermute | solution.py:370
  51.5 9.5 %collective-permute-start.6 = (bf16[2,512,256]{2,1,0:T(8,128)(2,1)S(1)}, bf16[2,512,256]{2,1,0:T(8,128)(2,1)S(1)}, u32[]{:S(2)}, u32[]{:S(2)}) collective-permute-start(bf16[2,512,256]{2,1,0:T(8,128)(2,1)S(1)} %collective-permute-done.3), channel_id=1, source_target_pairs={{0,2},{2,0},{8,10},{10,8},{16,18},{18,16},{24,26},{26,24},{28,30},... | collective-permute-start | bytes 1572872 | tf_op jit(solution)/shard_map/ppermute | solution.py:370
  53.6 9.2 %collective-permute-start.5 = (bf16[2,512,256]{2,1,0:T(8,128)(2,1)S(1)}, bf16[2,512,256]{2,1,0:T(8,128)(2,1)S(1)}, u32[]{:S(2)}, u32[]{:S(2)}) collective-permute-start(bf16[2,512,256]{2,1,0:T(8,128)(2,1)S(1)} %collective-permute-done.3), channel_id=1, source_target_pairs={{0,8},{8,16},{16,24},{24,28},{28,20},{20,12},{12,4},{4,0},{2,6},{1... | collective-permute-start | bytes 1572872 | tf_op jit(solution)/shard_map/ppermute | solution.py:368
  57.1 13.0 %collective-permute-start.17 = (bf16[2,512,256]{2,1,0:T(8,128)(2,1)S(1)}, bf16[2,512,256]{2,1,0:T(8,128)(2,1)S(1)}, u32[]{:S(2)}, u32[]{:S(2)}) collective-permute-start(bf16[2,512,256]{2,1,0:T(8,128)(2,1)S(1)} %collective-permute-done.15), channel_id=1, source_target_pairs={{0,2},{2,0},{8,10},{10,8},{16,18},{18,16},{24,26},{26,24},{28,30},... | collective-permute-start | bytes 1572872 | tf_op jit(solution)/shard_map/ppermute | solution.py:370
  59.2 6.7 %collective-permute-start.18 = (bf16[1,512,256]{2,1,0:T(8,128)(2,1)S(1)}, bf16[1,512,256]{2,1,0:T(8,128)(2,1)S(1)}, u32[]{:S(2)}, u32[]{:S(2)}) collective-permute-start(bf16[1,512,256]{2,1,0:T(8,128)(2,1)S(1)} %slice.7), channel_id=1, source_target_pairs={{0,8},{8,16},{16,24},{24,28},{28,20},{20,12},{12,4},{4,0},{2,6},{1... | collective-permute-start | bytes 786440 | tf_op jit(solution)/shard_map/ppermute | solution.py:368
  62.8 5.7 %collective-permute-start.8 = (bf16[1,512,256]{2,1,0:T(8,128)(2,1)S(1)}, bf16[1,512,256]{2,1,0:T(8,128)(2,1)S(1)}, u32[]{:S(2)}, u32[]{:S(2)}) collective-permute-start(bf16[1,512,256]{2,1,0:T(8,128)(2,1)S(1)} %slice.6), channel_id=1, source_target_pairs={{0,8},{8,16},{16,24},{24,28},{28,20},{20,12},{12,4},{4,0},{2,6},{1... | collective-permute-start | bytes 786440 | tf_op jit(solution)/shard_map/ppermute | solution.py:368
  64.2 7.9 %collective-permute-start.7 = (bf16[2,512,256]{2,1,0:T(8,128)(2,1)S(1)}, bf16[2,512,256]{2,1,0:T(8,128)(2,1)S(1)}, u32[]{:S(2)}, u32[]{:S(2)}) collective-permute-start(bf16[2,512,256]{2,1,0:T(8,128)(2,1)S(1)} %collective-permute-done.5), channel_id=1, source_target_pairs={{0,2},{2,0},{8,10},{10,8},{16,18},{18,16},{24,26},{26,24},{28,30},... | collective-permute-start | bytes 1572872 | tf_op jit(solution)/shard_map/ppermute | solution.py:370
  65.9 5.3 %collective-permute-start.19 = (bf16[1,512,256]{2,1,0:T(8,128)(2,1)S(1)}, bf16[1,512,256]{2,1,0:T(8,128)(2,1)S(1)}, u32[]{:S(2)}, u32[]{:S(2)}) collective-permute-start(bf16[1,512,256]{2,1,0:T(8,128)(2,1)S(1)} %collective-permute-done.18), channel_id=1, source_target_pairs={{0,2},{2,0},{8,10},{10,8},{16,18},{18,16},{24,26},{26,24},{28,30},... | collective-permute-start | bytes 786440 | tf_op jit(solution)/shard_map/ppermute | solution.py:370
  68.5 4.7 %collective-permute-start.9 = (bf16[1,512,256]{2,1,0:T(8,128)(2,1)S(1)}, bf16[1,512,256]{2,1,0:T(8,128)(2,1)S(1)}, u32[]{:S(2)}, u32[]{:S(2)}) collective-permute-start(bf16[1,512,256]{2,1,0:T(8,128)(2,1)S(1)} %collective-permute-done.8), channel_id=1, source_target_pairs={{0,2},{2,0},{8,10},{10,8},{16,18},{18,16},{24,26},{26,24},{28,30},... | collective-permute-start | bytes 786440 | tf_op jit(solution)/shard_map/ppermute | solution.py:370
  74.0 24.0 %copy-start.1 = (bf16[64,4,4096]{2,1,0:T(4,128)(2,1)S(1)}, bf16[64,4,4096]{2,1,0:T(4,128)(2,1)}, u32[]{:S(2)}) copy-start(bf16[64,4,4096]{2,1,0:T(4,128)(2,1)} %param.8) | copy-start | bytes 6291460
